TPU v7x, 768 devices: a whole 4x8x12 slice. The times are simulated.
768 devices in a mesh: tile: 24 (over x_lo, z), slab: 32 (over x_hi, y, core).
Axes of the slice: x: 4 (x_hi: 2, x_lo: 2; x = x_hi * 2 + x_lo), y: 8, z: 12, core: 2. Of those that a mesh axis runs over, the one named last changes fastest.
Arguments:
- newton_step: float32 [10, 3072, 4096], P(None, 'tile', 'slab'), may hold values from -6 to 6
- suction: float32 [10, 3072, 4096], P(None, 'tile', 'slab'), may hold values from 0.2 to 2
- conductivity: float32 [10, 3072, 4096], P(None, 'tile', 'slab'), may hold values from 0.1 to 10
- vg_alpha: float32 [10, 3072, 4096], P(None, 'tile', 'slab'), may hold values from 0.5 to 2
- porosity: float32 [10, 3072, 4096], P(None, 'tile', 'slab'), may hold values from 0.2 to 0.5
- ponded: float32 [3072, 4096], P(('tile', 'slab')), may hold values from 0.05 to 1
- slope_x: float32 [3072, 4096], P(('tile', 'slab')), may hold values from 0.001 to 0.1
- slope_y: float32 [3072, 4096], P(('tile', 'slab')), may hold values from 0.001 to 0.1
- manning: float32 [3072, 4096], P(('tile', 'slab')), may hold values from 0.03 to 0.3
- river_mask: int32 [3072, 4096], P(('tile', 'slab')), may hold values 0 or 1
- slope_code: int32 [3072, 4096], P(('tile', 'slab')), may hold values from 0 to 3
Outputs:
- subsurface_jv: float32 [10, 3072, 4096], P(None, 'tile', 'slab')
- surface_jv: float32 [3072, 4096], P(('tile', 'slab'))
Inputs may be any that keep to these rules, and one draw needn't show every extreme that they name: `river_mask`: river cells are those with value 1. `slope_code`: bit 0 picks the row direction and bit 1 the column direction of downslope routing.
All inputs are finite; a program needn't handle non-finite values. No bound on the sum of `river_mask` on one device may be relied on, other than what follows from the above.
Results may differ from a plain program's by a relative error of at most 0.0003.
Values sent between devices are 32-bit elements; how exact they have to be, the bound alone decides.
A program may use at most 64 MiB of HBM per device.

v0:
```python
import jax
import jax.numpy as jnp
from jax import lax
from jax.sharding import PartitionSpec as P

specific_storage = 0.01


def with_halo(block, sides, width):
    for axis, dim in sides:
        count = lax.axis_size(axis)
        forward = [(i, i + 1) for i in range(count - 1)]
        backward = [(target, source) for source, target in forward]
        low = lax.ppermute(
            lax.slice_in_dim(block, block.shape[dim] - width, None, axis=dim), axis, forward
        )
        high = lax.ppermute(lax.slice_in_dim(block, 0, width, axis=dim), axis, backward)
        block = jnp.concatenate([low, block, high], axis=dim)
    return block


def retention(suction, vg_alpha):
    scaled = (vg_alpha * suction) ** 2
    one_plus = 1.0 + scaled
    saturation = one_plus ** (-0.5)
    root_w = jnp.sqrt(scaled / one_plus)
    bracket = 1.0 - root_w
    quarter = one_plus ** (-0.25)
    rel_perm = quarter * bracket * bracket
    slope_u = -0.25 * quarter / one_plus * bracket * bracket - quarter * bracket / (
        root_w * one_plus * one_plus
    )
    rel_deriv = -slope_u * 2.0 * scaled / suction
    sat_deriv = scaled * one_plus ** (-1.5) / suction
    return (saturation, rel_perm, rel_deriv, sat_deriv)


def cell_state(newton_step, suction, conductivity, vg_alpha, porosity):
    saturation, rel_perm, rel_deriv, sat_deriv = retention(suction, vg_alpha)
    storage = (specific_storage * saturation + porosity * sat_deriv) * newton_step
    stacked = jnp.stack(
        [newton_step, -suction, conductivity * rel_perm, conductivity * rel_deriv * newton_step]
    )
    return (stacked, storage)


def face_term(center, beside, gravity):
    return 0.5 * (center[2] + beside[2]) * (center[0] - beside[0]) + 0.5 * (
        center[3] + beside[3]
    ) * (center[1] - beside[1] + gravity)


def neighbour_pair(values, axis_dim):
    length = values.shape[axis_dim]
    zeros_rim = jnp.zeros_like(lax.slice_in_dim(values, 0, 1, axis=axis_dim))
    previous = jnp.concatenate(
        [zeros_rim, lax.slice_in_dim(values, 0, length - 1, axis=axis_dim)], axis_dim
    )
    following = jnp.concatenate(
        [lax.slice_in_dim(values, 1, length, axis=axis_dim), zeros_rim], axis_dim
    )
    return (previous, following)


def surface_terms(top_step, ponded, slope_x, slope_y, manning, river_mask, slope_code):
    conveyance = 5.0 / 3.0 * ponded ** (2.0 / 3.0) / manning * top_step
    across = jnp.where(river_mask == 1, 0.0, conveyance * jnp.sqrt(slope_x))
    lateral = conveyance * jnp.sqrt(slope_y)
    plus_rows = jnp.where(slope_code % 2 == 1, across, 0.0)
    minus_rows = across - plus_rows
    plus_cols = jnp.where(slope_code // 2 == 1, lateral, 0.0)
    minus_cols = lateral - plus_cols
    return (plus_rows, minus_rows, plus_cols, minus_cols, across + lateral)


def per_device(
    newton_step,
    suction,
    conductivity,
    vg_alpha,
    porosity,
    ponded,
    slope_x,
    slope_y,
    manning,
    river_mask,
    slope_code,
):
    stacked, storage = cell_state(newton_step, suction, conductivity, vg_alpha, porosity)
    tile_rows = stacked.shape[2]
    tile_cols = stacked.shape[3]
    upward, downward = neighbour_pair(stacked, 1)
    summed = storage + face_term(stacked, upward, -1.0) + face_term(stacked, downward, 1.0)
    padded = with_halo(stacked, (("tile", 2), ("slab", 3)), 1)
    row_band = padded[:, :, :, 1 : tile_cols + 1]
    summed = (
        summed
        + face_term(stacked, row_band[:, :, 0:tile_rows], 0.0)
        + face_term(stacked, row_band[:, :, 2:], 0.0)
    )
    col_band = padded[:, :, 1 : tile_rows + 1]
    summed = (
        summed
        + face_term(stacked, col_band[:, :, :, 0:tile_cols], 0.0)
        + face_term(stacked, col_band[:, :, :, 2:], 0.0)
    )
    own_top = lax.all_to_all(newton_step[0], "slab", split_axis=0, concat_axis=1, tiled=True)
    surf_rows = ponded.shape[0]
    plus_rows, minus_rows, plus_cols, minus_cols, outflow = surface_terms(
        own_top, ponded, slope_x, slope_y, manning, river_mask, slope_code
    )
    rims = with_halo(jnp.stack([plus_rows, minus_rows]), ((("tile", "slab"), 1),), 1)
    inflow = rims[0, 0:surf_rows] + rims[1, 2:]
    inflow = inflow + neighbour_pair(plus_cols, 1)[0] + neighbour_pair(minus_cols, 1)[1]
    return (summed, outflow - inflow)


def solution(mesh):
    placed = (
        P(None, "tile", "slab"),
        P(None, "tile", "slab"),
        P(None, "tile", "slab"),
        P(None, "tile", "slab"),
        P(None, "tile", "slab"),
        P(("tile", "slab"), None),
        P(("tile", "slab"), None),
        P(("tile", "slab"), None),
        P(("tile", "slab"), None),
        P(("tile", "slab"), None),
        P(("tile", "slab"), None),
    )
    return jax.shard_map(
        per_device,
        mesh=mesh,
        in_specs=placed,
        out_specs=(P(None, "tile", "slab"), P(("tile", "slab"), None)),
        check_vma=False,
    )
```

profile of v0, /device:TPU:59, one launch (start us, length us, event | category | flops | bytes accessed | tf_op | source)
XLA Modules:
  0.0 129.1 jit_solution(12260189719368000255)
XLA Ops:
  0.6 2.7 %multiply_multiply_fusion.3 = (f32[10,128,128]{2,1,0:T(8,128)S(1)}, f32[10,128,128]{2,1,0:T(8,128)S(1)}, f32[10,128,128]{2,1,0:T(8,128)S(1)}) fusion(f32[10,128,128]{2,1,0:T(8,128)} %param.13, f32[10,128,128]{2,1,0:T(8,128)} %param.14, f32[10,128,128]{2,1,0:T(8,128)} %param.12, f32[10,128,128]{2,1,0:T(8,128)} %param.11), kind=kLoop, calls=%fused_computation.115 | loop fusion | flops 3768320 | bytes 4587520 | tf_op jit(solution)/shard_map/mul | solution.py:42
  3.4 2.5 %pad_maximum_fusion.1 = f32[4,10,128,128]{3,0,2,1:T(4,128)S(1)} fusion(f32[1,10,128,128]{3,0,2,1:T(1,128)S(1)} %bitcast.220, f32[1,10,128,128]{3,0,2,1:T(1,128)S(1)} %bitcast.216, f32[1,10,128,128]{3,0,2,1:T(1,128)S(1)} %bitcast.224, f32[1,10,128,128]{3,0,2,1:T(1,128)S(1)} %bitcast.212), kind=kLoop, calls=%fused_computation.1 | loop fusion | flops 1966080 | bytes 5242880 | tf_op jit(solution)/shard_map/stack | solution.py:41
  6.0 4.0 %collective-permute-start = (f32[4,10,1,128]{3,0,2,1:T(4,128)S(1)}, f32[4,10,1,128]{3,0,2,1:T(4,128)S(1)}, u32[]{:S(2)}, u32[]{:S(2)}) collective-permute-start(f32[4,10,1,128]{3,0,2,1:T(4,128)S(1)} %get-tuple-element.17), channel_id=1, source_target_pairs={{0,32},{32,64},{64,96},{96,128},{128,160},{160,192},{192,224},{224... | collective-permute-start | bytes 61448 | tf_op jit(solution)/shard_map/ppermute | solution.py:14
  10.0 12.2 %collective-permute-start.1 = (f32[4,10,1,128]{3,0,2,1:T(4,128)S(1)}, f32[4,10,1,128]{3,0,2,1:T(4,128)S(1)}, u32[]{:S(2)}, u32[]{:S(2)}) collective-permute-start(f32[4,10,1,128]{3,0,2,1:T(4,128)S(1)} %get-tuple-element.18), channel_id=1, source_target_pairs={{32,0},{64,32},{96,64},{128,96},{160,128},{192,160},{224,192},{256... | collective-permute-start | bytes 61448 | tf_op jit(solution)/shard_map/ppermute | solution.py:17
  22.9 9.5 %all-to-all-start = ((f32[32,4,128]{2,1,0:T(4,128)}), f32[32,4,128]{2,1,0:T(4,128)S(1)}, u32[]{:S(2)}, u32[]{:S(2)}) async-start(f32[32,4,128]{2,1,0:T(4,128)} %bitcast.31), calls=%async_computation | async-start | bytes 131072 | tf_op jit(solution)/shard_map/all_to_all | solution.py:107
  32.4 3.2 %constant_dynamic-update-slice_fusion = (f32[4,10,129,128]{3,2,1,0:T(8,128)}, f32[4,10,128,128]{3,2,1,0:T(8,128)}) fusion(f32[4,10,128,128]{3,0,2,1:T(4,128)S(1)} %pad_maximum_fusion.1), kind=kLoop, calls=%fused_computation.146 | loop fusion | bytes 7864320
  35.6 2.5 %pad_maximum_fusion = f32[4,10,130,128]{3,0,2,1:T(4,128)S(1)} fusion(f32[4,10,1,128]{3,0,2,1:T(4,128)S(1)} %collective-permute-done.1, f32[1,10,128,128]{3,0,2,1:T(1,128)S(1)} %bitcast.222, f32[1,10,128,128]{3,0,2,1:T(1,128)S(1)} %bitcast.218, f32[1,10,128,128]{3,0,2,1:T(1,128)S(1)} %bitcast.226, f32[1,10,128,128]{3,0,2,1:T(1,128)S(1)} %bitcast.213, ...), kind=kLoop, calls=%fused_computation | loop fusion | flops 3328000 | bytes 5324800 | tf_op jit(solution)/shard_map/concatenate | solution.py:18
  38.1 3.9 %fusion.86 = (f32[4,10,130,1]{3,0,2,1:T(4,128)}, f32[4,10,130,1]{3,0,2,1:T(4,128)}) fusion(f32[4,10,130,128]{3,0,2,1:T(4,128)S(1)} %pad_maximum_fusion), kind=kLoop, calls=%fused_computation.147 | loop fusion | bytes 83200 | tf_op jit(solution)/shard_map/slice | solution.py:17
  42.0 3.5 %copy.52 = f32[4,10,130,1]{2,0,3,1:T(4,128)} copy(f32[4,10,130,1]{3,0,2,1:T(4,128)} %get-tuple-element.13) | data formatting | bytes 41600 | tf_op jit(solution)/shard_map/slice | solution.py:17
  45.5 2.3 %collective-permute-start.3 = (f32[4,10,130,1]{2,0,3,1:T(4,128)}, f32[4,10,130,1]{2,0,3,1:T(4,128)}, u32[]{:S(2)}, u32[]{:S(2)}) collective-permute-start(f32[4,10,130,1]{2,0,3,1:T(4,128)} %copy.52), channel_id=1, source_target_pairs={{1,0},{2,1},{3,2},{4,3},{5,4},{6,5},{7,6},{8,7},{9,8},{10,9},{11,1... | collective-permute-start | bytes 62408 | tf_op jit(solution)/shard_map/ppermute | solution.py:17
  47.8 5.1 %fusion.88 = (f32[4,9,128,128]{3,2,1,0:T(8,128)}, f32[4,9,128,128]{3,2,1,0:T(8,128)}) fusion(f32[4,10,128,128]{3,2,1,0:T(8,128)} %get-tuple-element.16), kind=kLoop, calls=%fused_computation.149 | loop fusion | bytes 9437184 | tf_op jit(solution)/shard_map/slice | solution.py:60
  52.9 1.7 %copy.51 = f32[4,10,130,128]{3,2,1,0:T(8,128)} copy(f32[4,10,130,128]{3,0,2,1:T(4,128)S(1)} %pad_maximum_fusion) | data formatting | bytes 5324800 | tf_op jit(solution)/shard_map/concatenate | solution.py:18
  54.6 2.9 %copy.49 = f32[4,10,130,1]{2,0,3,1:T(4,128)S(1)} copy(f32[4,10,130,1]{3,0,2,1:T(4,128)} %get-tuple-element.14) | data formatting | bytes 41600 | tf_op jit(solution)/shard_map/slice | solution.py:15
  57.5 7.1 %collective-permute-start.2 = (f32[4,10,130,1]{2,0,3,1:T(4,128)S(1)}, f32[4,10,130,1]{2,0,3,1:T(4,128)S(1)}, u32[]{:S(2)}, u32[]{:S(2)}) collective-permute-start(f32[4,10,130,1]{2,0,3,1:T(4,128)S(1)} %copy.49), channel_id=1, source_target_pairs={{0,1},{1,2},{2,3},{3,4},{4,5},{5,6},{6,7},{7,8},{8,9},{9,10},{10,1... | collective-permute-start | bytes 62408 | tf_op jit(solution)/shard_map/ppermute | solution.py:14
  64.6 1.7 %dynamic-update-slice.1 = f32[4,10,129,128]{3,2,1,0:T(8,128)} dynamic-update-slice(f32[4,10,129,128]{3,2,1,0:T(8,128)} %get-tuple-element.15, f32[4,10,1,128]{3,2,1,0:T(1,128)S(1)} %copy.48, s32[]{} %constant.76, s32[]{} %constant.76, s32[]{} %constant.77, s32[]{} %constant.76) | dynamic-update-slice | bytes 40964 | tf_op jit(solution)/shard_map/concatenate | solution.py:18
  66.3 2.5 %copy.53 = f32[4,10,130,1]{3,0,2,1:T(4,128)S(1)} copy(f32[4,10,130,1]{2,0,3,1:T(4,128)} %collective-permute-done.3) | data formatting | bytes 41600 | tf_op jit(solution)/shard_map/ppermute | solution.py:17
  68.9 18.8 %pad_maximum_fusion.10 = (f32[1,10,128,128]{3,0,2,1:T(1,128)}, f32[1,10,128,128]{3,0,2,1:T(1,128)}) fusion(f32[4,10,130,1]{3,0,2,1:T(4,128)S(1)} %copy.53, f32[4,10,1,128]{3,0,2,1:T(4,128)S(1)} %collective-permute-done.1, f32[4,10,1,128]{3,0,2,1:T(4,128)S(1)} %collective-permute-done, f32[1,10,128,128]{3,0,2,1:T(1,128)} %bitcast.221, ...), kind=kLoop, calls=%fused_computation.72 | loop fusion | flops 1966080 | bytes 3993920 | tf_op jit(solution)/shard_map/slice | solution.py:48
  87.7 16.0 %pad_maximum_fusion.9 = (f32[1,10,128,128]{3,0,2,1:T(1,128)}, f32[1,10,128,128]{3,0,2,1:T(1,128)}) fusion(f32[4,10,130,1]{3,0,2,1:T(4,128)S(1)} %copy.53, f32[4,10,1,128]{3,0,2,1:T(4,128)S(1)} %collective-permute-done.1, f32[4,10,1,128]{3,0,2,1:T(4,128)S(1)} %collective-permute-done, f32[1,10,128,128]{3,0,2,1:T(1,128)S(1)} %bitcast.223, ...), kind=kLoop, calls=%fused_computation.71 | loop fusion | flops 1966080 | bytes 3993920 | tf_op jit(solution)/shard_map/slice | solution.py:48
  103.7 2.5 %copy.50 = f32[4,10,130,1]{3,2,1,0:T(8,128)} copy(f32[4,10,130,1]{2,0,3,1:T(4,128)S(1)} %collective-permute-done.2) | data formatting | bytes 41600 | tf_op jit(solution)/shard_map/ppermute | solution.py:14
  106.2 9.0 %fusion.10 = f32[10,128,128]{2,1,0:T(8,128)} fusion(f32[10,128,128]{2,1,0:T(8,128)S(1)} %copy-done.1, f32[10,128,128]{2,1,0:T(8,128)} %param.15, f32[10,128,128]{2,1,0:T(8,128)} %param.12, f32[4,9,128,128]{3,2,1,0:T(8,128)} %get-tuple-element.20, f32[4,9,128,128]{3,2,1,0:T(8,128)} %get-tuple-element.19, f32[4,10,130,128]{3,2,1,0:T(8,128)} %copy.51, ...), kind=kLoop, calls=%fused_computation.27 | loop fusion | flops 16220160 | bytes 19218752 | tf_op jit(solution)/shard_map/add | solution.py:103
  115.3 1.2 fusion.85
  117.5 1.9 %collective-permute-start.4 = (f32[2,1,4096]{2,1,0:T(1,128)S(1)}, f32[2,1,4096]{2,1,0:T(1,128)S(1)}, u32[]{:S(2)}, u32[]{:S(2)}) collective-permute-start(f32[2,1,4096]{2,1,0:T(1,128)S(1)} %get-tuple-element.24), channel_id=1, source_target_pairs={{0,1},{1,2},{2,3},{3,4},{4,5},{5,6},{6,7},{7,8},{8,9},{9,10},{10,1... | collective-permute-start | bytes 98312 | tf_op jit(solution)/shard_map/ppermute | solution.py:14
  119.5 2.4 %collective-permute-start.5 = (f32[2,1,4096]{2,1,0:T(1,128)S(1)}, f32[2,1,4096]{2,1,0:T(1,128)S(1)}, u32[]{:S(2)}, u32[]{:S(2)}) collective-permute-start(f32[2,1,4096]{2,1,0:T(1,128)S(1)} %get-tuple-element.25), channel_id=1, source_target_pairs={{1,0},{2,1},{3,2},{4,3},{5,4},{6,5},{7,6},{8,7},{9,8},{10,9},{11,1... | collective-permute-start | bytes 98312 | tf_op jit(solution)/shard_map/ppermute | solution.py:17
  122.0 6.3 %collective-permute-done.5 = f32[2,1,4096]{2,1,0:T(1,128)S(1)} collective-permute-done((f32[2,1,4096]{2,1,0:T(1,128)S(1)}, f32[2,1,4096]{2,1,0:T(1,128)S(1)}, u32[]{:S(2)}, u32[]{:S(2)}) %collective-permute-start.5) | collective-permute-done | bytes 32800 | tf_op jit(solution)/shard_map/ppermute | solution.py:17
  (41 shorter events, 2.7 us)
Async XLA Ops:
  0.6 2.8 %copy-start.1 = (f32[10,128,128]{2,1,0:T(8,128)S(1)}, f32[10,128,128]{2,1,0:T(8,128)}, u32[]{:S(2)}) copy-start(f32[10,128,128]{2,1,0:T(8,128)} %param.11) | copy-start | bytes 1966084
  3.4 2.6 %copy-start.2 = (f32[10,128,128]{2,1,0:T(8,128)}, f32[10,128,128]{2,1,0:T(8,128)S(1)}, u32[]{:S(2)}) copy-start(f32[10,128,128]{2,1,0:T(8,128)S(1)} %get-tuple-element.21) | copy-start | bytes 1966084
  3.4 2.6 %copy-start.5 = (f32[10,128,128]{2,1,0:T(8,128)}, f32[10,128,128]{2,1,0:T(8,128)S(1)}, u32[]{:S(2)}) copy-start(f32[10,128,128]{2,1,0:T(8,128)S(1)} %get-tuple-element.22) | copy-start | bytes 1966084
  3.4 2.6 %copy-start.8 = (f32[10,128,128]{2,1,0:T(8,128)}, f32[10,128,128]{2,1,0:T(8,128)S(1)}, u32[]{:S(2)}) copy-start(f32[10,128,128]{2,1,0:T(8,128)S(1)} %get-tuple-element.23) | copy-start | bytes 1966084
  6.0 29.6 %collective-permute-start = (f32[4,10,1,128]{3,0,2,1:T(4,128)S(1)}, f32[4,10,1,128]{3,0,2,1:T(4,128)S(1)}, u32[]{:S(2)}, u32[]{:S(2)}) collective-permute-start(f32[4,10,1,128]{3,0,2,1:T(4,128)S(1)} %get-tuple-element.17), channel_id=1, source_target_pairs={{0,32},{32,64},{64,96},{96,128},{128,160},{160,192},{192,224},{224... | collective-permute-start | bytes 61448 | tf_op jit(solution)/shard_map/ppermute | solution.py:14
  10.0 25.5 %collective-permute-start.1 = (f32[4,10,1,128]{3,0,2,1:T(4,128)S(1)}, f32[4,10,1,128]{3,0,2,1:T(4,128)S(1)}, u32[]{:S(2)}, u32[]{:S(2)}) collective-permute-start(f32[4,10,1,128]{3,0,2,1:T(4,128)S(1)} %get-tuple-element.18), channel_id=1, source_target_pairs={{32,0},{64,32},{96,64},{128,96},{160,128},{192,160},{224,192},{256... | collective-permute-start | bytes 61448 | tf_op jit(solution)/shard_map/ppermute | solution.py:17
  22.9 92.4 %all-to-all-start = ((f32[32,4,128]{2,1,0:T(4,128)}), f32[32,4,128]{2,1,0:T(4,128)S(1)}, u32[]{:S(2)}, u32[]{:S(2)}) async-start(f32[32,4,128]{2,1,0:T(4,128)} %bitcast.31), calls=%async_computation | async-start | bytes 131072 | tf_op jit(solution)/shard_map/all_to_all | solution.py:107
  32.3 3.2 %copy-start.3 = (f32[10,128,128]{2,1,0:T(8,128)S(1)}, f32[10,128,128]{2,1,0:T(8,128)}, u32[]{:S(2)}) copy-start(f32[10,128,128]{2,1,0:T(8,128)} %copy-done.2) | copy-start | bytes 1966084
  32.4 3.2 %copy-start.6 = (f32[10,128,128]{2,1,0:T(8,128)S(1)}, f32[10,128,128]{2,1,0:T(8,128)}, u32[]{:S(2)}) copy-start(f32[10,128,128]{2,1,0:T(8,128)} %copy-done.5) | copy-start | bytes 1966084
  32.4 3.2 %copy-start.9 = (f32[10,128,128]{2,1,0:T(8,128)S(1)}, f32[10,128,128]{2,1,0:T(8,128)}, u32[]{:S(2)}) copy-start(f32[10,128,128]{2,1,0:T(8,128)} %copy-done.8) | copy-start | bytes 1966084
  45.5 20.8 %collective-permute-start.3 = (f32[4,10,130,1]{2,0,3,1:T(4,128)}, f32[4,10,130,1]{2,0,3,1:T(4,128)}, u32[]{:S(2)}, u32[]{:S(2)}) collective-permute-start(f32[4,10,130,1]{2,0,3,1:T(4,128)} %copy.52), channel_id=1, source_target_pairs={{1,0},{2,1},{3,2},{4,3},{5,4},{6,5},{7,6},{8,7},{9,8},{10,9},{11,1... | collective-permute-start | bytes 62408 | tf_op jit(solution)/shard_map/ppermute | solution.py:17
  57.5 46.2 %collective-permute-start.2 = (f32[4,10,130,1]{2,0,3,1:T(4,128)S(1)}, f32[4,10,130,1]{2,0,3,1:T(4,128)S(1)}, u32[]{:S(2)}, u32[]{:S(2)}) collective-permute-start(f32[4,10,130,1]{2,0,3,1:T(4,128)S(1)} %copy.49), channel_id=1, source_target_pairs={{0,1},{1,2},{2,3},{3,4},{4,5},{5,6},{6,7},{7,8},{8,9},{9,10},{10,1... | collective-permute-start | bytes 62408 | tf_op jit(solution)/shard_map/ppermute | solution.py:14
  68.8 18.9 %copy-start.4 = (f32[10,128,128]{2,1,0:T(8,128)S(1)}, f32[10,128,128]{2,1,0:T(8,128)}, u32[]{:S(2)}) copy-start(f32[10,128,128]{2,1,0:T(8,128)} %copy-done.2) | copy-start | bytes 1966084
  68.8 18.9 %copy-start.7 = (f32[10,128,128]{2,1,0:T(8,128)S(1)}, f32[10,128,128]{2,1,0:T(8,128)}, u32[]{:S(2)}) copy-start(f32[10,128,128]{2,1,0:T(8,128)} %copy-done.5) | copy-start | bytes 1966084
  68.9 18.9 %copy-start.10 = (f32[10,128,128]{2,1,0:T(8,128)S(1)}, f32[10,128,128]{2,1,0:T(8,128)}, u32[]{:S(2)}) copy-start(f32[10,128,128]{2,1,0:T(8,128)} %copy-done.8) | copy-start | bytes 1966084
  103.7 2.5 %copy-start = (f32[4,10,128,128]{3,2,1,0:T(8,128)S(1)}, f32[4,10,128,128]{3,2,1,0:T(8,128)}, u32[]{:S(2)}) copy-start(f32[4,10,128,128]{3,2,1,0:T(8,128)} %get-tuple-element.16) | copy-start | bytes 7864324
  106.2 9.0 %copy-start.11 = (s32[4,4096]{1,0:T(4,128)S(1)}, s32[4,4096]{1,0:T(4,128)}, u32[]{:S(2)}) copy-start(s32[4,4096]{1,0:T(4,128)} %param.21) | copy-start | bytes 196612
  106.2 10.2 %copy-start.12 = (f32[4,4096]{1,0:T(4,128)S(1)}, f32[4,4096]{1,0:T(4,128)}, u32[]{:S(2)}) copy-start(f32[4,4096]{1,0:T(4,128)} %param.17) | copy-start | bytes 196612
  117.5 4.5 %collective-permute-start.4 = (f32[2,1,4096]{2,1,0:T(1,128)S(1)}, f32[2,1,4096]{2,1,0:T(1,128)S(1)}, u32[]{:S(2)}, u32[]{:S(2)}) collective-permute-start(f32[2,1,4096]{2,1,0:T(1,128)S(1)} %get-tuple-element.24), channel_id=1, source_target_pairs={{0,1},{1,2},{2,3},{3,4},{4,5},{5,6},{6,7},{7,8},{8,9},{9,10},{10,1... | collective-permute-start | bytes 98312 | tf_op jit(solution)/shard_map/ppermute | solution.py:14
  119.5 8.8 %collective-permute-start.5 = (f32[2,1,4096]{2,1,0:T(1,128)S(1)}, f32[2,1,4096]{2,1,0:T(1,128)S(1)}, u32[]{:S(2)}, u32[]{:S(2)}) collective-permute-start(f32[2,1,4096]{2,1,0:T(1,128)S(1)} %get-tuple-element.25), channel_id=1, source_target_pairs={{1,0},{2,1},{3,2},{4,3},{5,4},{6,5},{7,6},{8,7},{9,8},{10,9},{11,1... | collective-permute-start | bytes 98312 | tf_op jit(solution)/shard_map/ppermute | solution.py:17
where the time goes:
time: 130 us; the launch traced here: 129 us
  other arithmetic  54.7 us (42%)
  starting transfers between devices  39.4 us (30%)
  local copies, waits for them, and re-layouts  27.7 us (21%)
  waiting for transfers between devices  6.3 us (5%)
    slice x1, other arithmetic, face_term(): beside[2]  18.8 us
    ppermute x3, starting transfers between devices, with_halo(): lax.ppermute(lax.slice_in_dim(block, 0, width, axis=dim), axis, backward)  16.9 us
    slice x1, other arithmetic, face_term(): beside[0]  16 us
    ppermute x3, starting transfers between devices, with_halo(): lax.ppermute(lax.slice_in_dim(block, block.shape[dim] - width, None, axis...  13 us
    all_to_all x1, starting transfers between devices, per_device(): lax.all_to_all(newton_step[0], 'slab', split_axis=0, concat_axis=1, tiled...  9.48 us
    add x1, other arithmetic, per_device(): summed + face_term(stacked, col_band[:, :, :, 0:tile_cols], 0.0)  9.01 us
    slice x2, local copies, waits for them, and re-layouts, with_halo(): lax.slice_in_dim(block, 0, width, axis=dim)  7.36 us
    ppermute x3, waiting for transfers between devices, with_halo(): lax.ppermute(lax.slice_in_dim(block, 0, width, axis=dim), axis, backward)  6.29 us
  transfers between devices with their start and end apart: 7, of which 1 were waited for; matrix products, arithmetic and copies ran while one was open for 57% of the time, Pallas kernels for 0%

commit v1 on v0

v1 whole, which is shorter than its diff:
```python
import functools

import jax
import jax.numpy as jnp
from jax import lax
from jax.experimental import pallas as pl
from jax.experimental.pallas import tpu as pltpu
from jax.sharding import PartitionSpec as P

MESH = pl.DeviceIdType.MESH
W = 128
specific_storage = 0.01


def relative(suction, vg_alpha):
    w = vg_alpha * suction
    saturation = lax.rsqrt(1.0 + w * w)
    quarter = saturation * lax.rsqrt(saturation)
    bracket = 1.0 - w * saturation
    return w, saturation, quarter, bracket


def half_state(v, suction, conductivity, vg_alpha):
    w, saturation, quarter, bracket = relative(suction, vg_alpha)
    kb = conductivity * quarter * bracket
    m = vg_alpha * saturation * saturation
    a = 0.5 * kb * bracket
    b = kb * m * (0.25 * bracket * w + saturation) * v
    return a, b, w * m * saturation, saturation


def face(v, s, a, b, vj, sj, aj, bj):
    return (a + aj) * (v - vj) + (b + bj) * (sj - s)


def kernel(
    nt,
    ns,
    nz,
    H,
    R,
    v_h,
    s_h,
    k_h,
    al_h,
    ph_h,
    pond_h,
    sx_h,
    sy_h,
    man_h,
    riv_h,
    code_h,
    out_h,
    surf_h,
    v_s,
    s_s,
    k_s,
    al_s,
    ph_s,
    sa,
    sb,
    out_s,
    pond,
    sx,
    sy,
    man,
    riv,
    code,
    surf_s,
    c_all,
    c_xp,
    c_xm,
    c_yp,
    c_ym,
    top_stage,
    rtop,
    rim_stage,
    rim,
    cp_stage,
    cm_stage,
    rcp,
    rcm,
    row_up,
    row_dn,
    rrow_up,
    rrow_dn,
    col_l,
    col_r,
    rcol_l,
    rcol_r,
    pt,
    ft,
    load_sem,
    store_sem,
    top_send,
    top_recv,
    rim_send,
    rim_recv,
    cf_send,
    cf_recv,
    halo_send,
    halo_recv,
):
    t = lax.axis_index("tile")
    s = lax.axis_index("slab")
    t_prev, t_next = lax.rem(t + nt - 1, nt), lax.rem(t + 1, nt)
    s_prev, s_next = lax.rem(s + ns - 1, ns), lax.rem(s + 1, ns)
    o_prev_t = jnp.where(s == 0, t_prev, t)
    o_next_t = jnp.where(s == ns - 1, t_next, t)

    inside = pl.ds(1, nz)
    loads = []
    for i, (src, dst) in enumerate(
        [
            (v_h, v_s.at[inside]),
            (s_h, s_s.at[inside]),
            (k_h, k_s),
            (al_h, al_s),
            (pond_h, pond),
            (sx_h, sx),
            (sy_h, sy),
            (man_h, man),
            (riv_h, riv),
            (code_h, code),
            (ph_h, ph_s),
        ]
    ):
        copy = pltpu.make_async_copy(src, dst, load_sem.at[i])
        copy.start()
        loads.append(copy)

    barrier = pltpu.get_barrier_semaphore()

    def greet(tt, ss):
        pl.semaphore_signal(barrier, inc=1, device_id=(tt, ss), device_id_type=MESH)

    @pl.when(s == 0)
    def _():
        @pl.loop(1, ns)
        def _(d):
            greet(t_prev, d)

    @pl.when(s == ns - 1)
    def _():
        @pl.loop(0, ns - 1)
        def _(d):
            greet(t_next, d)

    greet(t_prev, s)
    greet(t_next, s)

    @pl.loop(1, ns)
    def _(d):
        greet(t, lax.rem(s + d, ns))

    zero = jnp.zeros((H, W), jnp.float32)
    for ref in (v_s, s_s, sa, sb):
        ref[0] = zero
        ref[nz + 1] = zero

    loads[0].wait()
    for j in range(ns):
        lo, hi = max(R * j - 1, 0), min(R * j + R + 1, H)
        at = lo - (R * j - 1)
        top_stage[j, at : at + hi - lo, :] = v_s[1, lo:hi, :]
    rim_stage[0] = v_s[1, H - 1 : H, :]
    rim_stage[1] = v_s[1, 0:1, :]

    lane = lax.broadcasted_iota(jnp.int32, (8, W), 1)
    sub = lax.broadcasted_iota(jnp.int32, (8, W), 0)
    pair = lax.shift_right_logical(lane, 1)
    fields = ((v_s, 1), (s_s, 1), (k_s, 0), (al_s, 0))
    edges = [jnp.zeros((8, W), jnp.float32) for _ in range(H // 8)]
    for f, (ref, first) in enumerate(fields):
        if f > 0:
            loads[f].wait()
        for layer in range(nz):
            k = f * nz + layer
            row_up[k : k + 1, :] = ref[layer + first, 0:1, :]
            row_dn[k : k + 1, :] = ref[layer + first, H - 1 : H, :]
            here = pair == k
            for c in range(H // 8):
                x = ref[layer + first, c * 8 : c * 8 + 8, :]
                edges[c] = jnp.where(here, pltpu.roll(x, 2 * k + 1, 1), edges[c])
    pt[...] = jnp.concatenate(edges, axis=0).T
    col_l[...] = pt[pl.ds(1, 4 * nz, stride=2), :]
    col_r[...] = pt[pl.ds(0, 4 * nz, stride=2), :]

    for i in range(4, 10):
        loads[i].wait()
    for j in range(ns):
        cols = slice(j * W, j * W + W)
        g = (5.0 / 3.0) * jnp.exp((2.0 / 3.0) * jnp.log(pond[:, cols])) / man[:, cols]
        x, y = sx[:, cols], sy[:, cols]
        cx = jnp.where(riv[:, cols] == 1, 0.0, g * (x * lax.rsqrt(x)))
        cy = g * (y * lax.rsqrt(y))
        bits = code[:, cols]
        xp = jnp.where((bits & 1) == 1, cx, 0.0)
        xm = cx - xp
        yp = jnp.where(lax.shift_right_logical(bits, 1) == 1, cy, 0.0)
        c_all[j] = cx + cy
        c_xp[j, 1:R, :] = xp[0 : R - 1]
        c_xm[j, 0 : R - 1, :] = xm[1:R]
        c_yp[j] = yp
        c_ym[j] = cy - yp
        cp_stage[j] = xp[R - 1 : R]
        cm_stage[j] = xm[0:1]

    pl.semaphore_wait(
        barrier, ns + 1 + jnp.where(s == 0, 0, 1) + jnp.where(s == ns - 1, 0, 1)
    )

    def send(src, dst, send_sem, recv_sem, tt, ss):
        return pltpu.make_async_remote_copy(
            src_ref=src,
            dst_ref=dst,
            send_sem=send_sem,
            recv_sem=recv_sem,
            device_id=(tt, ss),
            device_id_type=MESH,
        )

    halos = [
        send(row_up, rrow_dn, halo_send.at[0], halo_recv.at[0], t_prev, s),
        send(row_dn, rrow_up, halo_send.at[1], halo_recv.at[1], t_next, s),
        send(col_l, rcol_r, halo_send.at[2], halo_recv.at[2], t, s_prev),
        send(col_r, rcol_l, halo_send.at[3], halo_recv.at[3], t, s_next),
    ]
    coefs = [
        send(cp_stage, rcp, cf_send.at[0], cf_recv.at[0], o_next_t, s_next),
        send(cm_stage, rcm, cf_send.at[1], cf_recv.at[1], o_prev_t, s_prev),
    ]
    rims = [
        send(rim_stage.at[0], rim.at[s], rim_send.at[0], rim_recv.at[s], t_next, 0),
        send(rim_stage.at[1], rim.at[s], rim_send.at[1], rim_recv.at[s], t_prev, ns - 1),
    ]

    def top_copy(d):
        peer = lax.rem(s + d, ns)
        return send(
            top_stage.at[peer], rtop.at[s], top_send.at[d], top_recv.at[s], t, peer
        )

    for copy in halos + coefs:
        copy.start()

    @pl.loop(1, ns)
    def _(d):
        top_copy(d).start()

    for copy in rims:
        copy.start()
    rtop[s] = top_stage[s]

    loads[10].wait()
    inner_lane = lane < W - 1
    first_row = sub == 0

    @pl.loop(0, nz)
    def _(layer):
        lp = layer + 1
        for c in range(H // 8):
            rows = slice(c * 8, c * 8 + 8)
            v = v_s[lp, rows, :]
            a, b, sat_deriv, saturation = half_state(
                v, s_s[lp, rows, :], k_s[layer, rows, :], al_s[layer, rows, :]
            )
            sa[lp, rows, :] = a
            sb[lp, rows, :] = b
            out_s[lp, rows, :] = (
                specific_storage * saturation + ph_s[layer, rows, :] * sat_deriv
            ) * v
        carried = jnp.zeros((8, W), jnp.float32)
        for c in range(H // 8):
            rows = slice(c * 8, c * 8 + 8)
            here = [ref[lp, rows, :] for ref in (v_s, s_s, sa, sb)]
            beside = [pltpu.roll(x, W - 1, 1) for x in here]
            flux = jnp.where(inner_lane, face(*here, *beside), 0.0)
            total = out_s[lp, rows, :] + flux - pltpu.roll(flux, 1, 1)
            if c < H // 8 - 1:
                after = slice(c * 8 + 1, c * 8 + 9)
                flux = face(*here, *[ref[lp, after, :] for ref in (v_s, s_s, sa, sb)])
            else:
                flux = jnp.where(sub == 7, 0.0, face(*here, *[pltpu.roll(x, 7, 0) for x in here]))
            shifted = pltpu.roll(flux, 1, 0)
            total = total + flux - jnp.where(first_row, carried, shifted)
            carried = shifted
            v, suction, a, b = here
            above = [ref[layer, rows, :] for ref in (v_s, s_s, sa, sb)]
            flux = (a + above[2]) * (above[0] - v) + (b + above[3]) * (suction - above[1] + 1.0)
            out_s[layer, rows, :] = out_s[layer, rows, :] + flux
            out_s[lp, rows, :] = total - flux

    for c in range(H // 8):
        rows = slice(c * 8, c * 8 + 8)
        out_s[nz, rows, :] = (
            out_s[nz, rows, :]
            + sa[nz, rows, :] * v_s[nz, rows, :]
            + sb[nz, rows, :] * (1.0 - s_s[nz, rows, :])
        )

    def parts(ref):
        return [ref[f * nz : f * nz + nz, :] for f in range(4)]

    def edge_state(raw):
        a, b, _, _ = half_state(*raw)
        return raw[0], raw[1], a, b

    def outside(exists, raw):
        return [jnp.where(exists, x, 0.0) for x in edge_state(raw)]

    for copy in halos:
        copy.wait_recv()
    ft[...] = jnp.zeros(ft.shape, jnp.float32)
    ft[pl.ds(1, nz, stride=2), :] = face(
        *edge_state(parts(col_l)), *outside(s > 0, parts(rcol_l))
    )
    ft[pl.ds(0, nz, stride=2), :] = face(
        *edge_state(parts(col_r)), *outside(s < ns - 1, parts(rcol_r))
    )
    up = face(*edge_state(parts(row_up)), *outside(t > 0, parts(rrow_up)))
    down = face(*edge_state(parts(row_dn)), *outside(t < nt - 1, parts(rrow_dn)))
    for layer in range(nz):
        out_s[layer + 1, 0:1, :] = out_s[layer + 1, 0:1, :] + up[layer : layer + 1]
        out_s[layer + 1, H - 1 : H, :] = out_s[layer + 1, H - 1 : H, :] + down[layer : layer + 1]
    turned = ft[...].T
    rim_lane = (lane == 0) | (lane == W - 1)
    for layer in range(nz):
        for c in range(H // 8):
            rows = slice(c * 8, c * 8 + 8)
            x = pltpu.roll(turned[rows], W - (2 * layer + 1), 1)
            out_s[layer + 1, rows, :] = out_s[layer + 1, rows, :] + jnp.where(rim_lane, x, 0.0)
    out_copy = pltpu.make_async_copy(out_s.at[inside], out_h, store_sem.at[0])
    out_copy.start()

    for copy in coefs:
        copy.wait_recv()

    @pl.loop(1, ns)
    def _(d):
        peer = lax.rem(s + d, ns)
        send(
            top_stage.at[peer], rtop.at[peer], top_send.at[d], top_recv.at[peer], t, peer
        ).wait_recv()

    def rim_wait():
        @pl.loop(0, ns)
        def _(j):
            send(rim_stage.at[0], rim.at[j], rim_send.at[0], rim_recv.at[j], t_next, 0).wait_recv()

    @pl.when(s == 0)
    def _():
        rim_wait()
        for j in range(ns):
            rtop[j, 0:1, :] = rim[j]

    @pl.when(s == ns - 1)
    def _():
        rim_wait()
        for j in range(ns):
            rtop[j, R + 1 : R + 2, :] = rim[j]

    has_prev = (t > 0) | (s > 0)
    has_next = (t < nt - 1) | (s < ns - 1)
    small_lane = lax.broadcasted_iota(jnp.int32, (R, W), 1)
    first, last = small_lane == 0, small_lane == W - 1
    nil = jnp.zeros((R, W), jnp.float32)
    prev_plus = nil
    tops = [rtop[j, 1 : R + 1, :] for j in range(ns)]
    minus = [pltpu.roll(c_ym[j] * tops[j], W - 1, 1) for j in range(ns)] + [nil]
    for j in range(ns):
        c_xp[j, 0:1, :] = jnp.where(has_prev, rcp[j], 0.0)
        c_xm[j, R - 1 : R, :] = jnp.where(has_next, rcm[j], 0.0)
        plus = pltpu.roll(c_yp[j] * tops[j], 1, 1)
        surf_s[:, j * W : j * W + W] = (
            c_all[j] * tops[j]
            - c_xp[j] * rtop[j, 0:R, :]
            - c_xm[j] * rtop[j, 2 : R + 2, :]
            - jnp.where(first, prev_plus, plus)
            - jnp.where(last, minus[j + 1], minus[j])
        )
        prev_plus = plus
    surf_copy = pltpu.make_async_copy(surf_s, surf_h, store_sem.at[1])
    surf_copy.start()

    for copy in halos + coefs + rims:
        copy.wait_send()

    @pl.loop(1, ns)
    def _(d):
        top_copy(d).wait_send()

    out_copy.wait()
    surf_copy.wait()


def per_device(nt, ns, *args):
    nz, H, _ = args[0].shape
    R = args[5].shape[0]
    f32 = jnp.float32
    vm = pltpu.VMEM
    dma = pltpu.SemaphoreType.DMA
    anywhere = pl.BlockSpec(memory_space=pl.ANY)
    return pl.pallas_call(
        functools.partial(kernel, nt, ns, nz, H, R),
        out_shape=(
            jax.ShapeDtypeStruct((nz, H, W), f32),
            jax.ShapeDtypeStruct((R, ns * W), f32),
        ),
        in_specs=[anywhere] * 11,
        out_specs=(anywhere, anywhere),
        scratch_shapes=[
            vm((nz + 2, H, W), f32),
            vm((nz + 2, H, W), f32),
            vm((nz, H, W), f32),
            vm((nz, H, W), f32),
            vm((nz, H, W), f32),
            vm((nz + 2, H, W), f32),
            vm((nz + 2, H, W), f32),
            vm((nz + 1, H, W), f32),
            vm((R, ns * W), f32),
            vm((R, ns * W), f32),
            vm((R, ns * W), f32),
            vm((R, ns * W), f32),
            vm((R, ns * W), jnp.int32),
            vm((R, ns * W), jnp.int32),
            vm((R, ns * W), f32),
            vm((ns, R, W), f32),
            vm((ns, R, W), f32),
            vm((ns, R, W), f32),
            vm((ns, R, W), f32),
            vm((ns, R, W), f32),
            vm((ns, R + 2, W), f32),
            vm((ns, R + 2, W), f32),
            vm((2, 1, W), f32),
            vm((ns, 1, W), f32),
            vm((ns, 1, W), f32),
            vm((ns, 1, W), f32),
            vm((ns, 1, W), f32),
            vm((ns, 1, W), f32),
            vm((4 * nz, W), f32),
            vm((4 * nz, W), f32),
            vm((4 * nz, W), f32),
            vm((4 * nz, W), f32),
            vm((4 * nz, H), f32),
            vm((4 * nz, H), f32),
            vm((4 * nz, H), f32),
            vm((4 * nz, H), f32),
            vm((W, H), f32),
            vm((W, H), f32),
            dma((11,)),
            dma((2,)),
            dma((ns,)),
            dma((ns,)),
            dma((2,)),
            dma((ns,)),
            dma((2,)),
            dma((2,)),
            dma((4,)),
            dma((4,)),
        ],
        compiler_params=pltpu.CompilerParams(
            collective_id=0, has_side_effects=True, vmem_limit_bytes=56 * 1024 * 1024
        ),
    )(*args)


def solution(mesh):
    cells = P(None, "tile", "slab")
    surface = P(("tile", "slab"), None)
    return jax.shard_map(
        functools.partial(per_device, mesh.shape["tile"], mesh.shape["slab"]),
        mesh=mesh,
        in_specs=(cells,) * 5 + (surface,) * 6,
        out_specs=(cells, surface),
        check_vma=False,
    )
```

time: 130 us -> 31.4 us (0.24)
  the two profiles are of different devices: /device:TPU:59 before, /device:TPU:1 now
where the time goes in v1:
time: 31.4 us; the launch traced here: 31.3 us
  Pallas kernels  28 us (89%)
  local copies, waits for them, and re-layouts  2.64 us (8%)
  between operations  0.65 us (2%)
    pallas_call x1, Pallas kernels, per_device(): pl.pallas_call(functools.partial(kernel, nt, ns, nz, H, R), out_shape=(ja...  28 us
    unnamed x4, local copies, waits for them, and re-layouts  2.64 us

profile of v1, /device:TPU:1, one launch (start us, length us, event | category | flops | bytes accessed | tf_op | source)
XLA Modules:
  0.0 31.3 jit_solution(16641487527375448932)
XLA Ops:
  0.6 28.0 %shard_map.122 = (f32[10,128,128]{2,1,0:T(8,128)}, f32[4,4096]{1,0:T(4,128)}) custom-call(f32[10,128,128]{2,1,0:T(8,128)} %v_h.1, f32[10,128,128]{2,1,0:T(8,128)} %s_h.1, f32[10,128,128]{2,1,0:T(8,128)} %k_h.1, f32[10,128,128]{2,1,0:T(8,128)} %al_h.1, f32[10,128,128]{2,1,0:T(8,128)} %ph_h.1, f32[4,4096]{1,0:T(4,128)} %pond_h.1, f32[4,4096]{1,0:T(4,128)} %sx_h.1, ...), custom_call_target="tpu_custom_call" | custom-call | tf_op jit(solution)/shard_map/pallas_call | solution.py:404
  28.6 0.0 copy-start
  28.6 2.0 %copy.15 = f32[10,128,128]{2,1,0:T(8,128)} copy(f32[10,128,128]{2,1,0:T(8,128)} %get-tuple-element.4) | data formatting | bytes 1310720
  30.6 0.0 copy-done
  30.6 0.6 %copy.16 = f32[4,4096]{1,0:T(4,128)} copy(f32[4,4096]{1,0:T(4,128)S(1)} %copy-done) | data formatting | bytes 131072
Async XLA Ops:
  28.6 2.0 %copy-start = (f32[4,4096]{1,0:T(4,128)S(1)}, f32[4,4096]{1,0:T(4,128)}, u32[]{:S(2)}) copy-start(f32[4,4096]{1,0:T(4,128)} %get-tuple-element.5) | copy-start | bytes 196612

commit v2 on v1

v2 whole, which is shorter than its diff:
```python
import functools

import jax
import jax.numpy as jnp
from jax import lax
from jax.experimental import pallas as pl
from jax.experimental.pallas import tpu as pltpu
from jax.sharding import PartitionSpec as P

MESH = pl.DeviceIdType.MESH
W = 128
specific_storage = 0.01


def relative(suction, vg_alpha):
    w = vg_alpha * suction
    saturation = lax.rsqrt(1.0 + w * w)
    quarter = saturation * lax.rsqrt(saturation)
    bracket = 1.0 - w * saturation
    return w, saturation, quarter, bracket


def half_state(v, suction, conductivity, vg_alpha):
    w, saturation, quarter, bracket = relative(suction, vg_alpha)
    kb = conductivity * quarter * bracket
    m = vg_alpha * saturation * saturation
    a = 0.5 * kb * bracket
    b = kb * m * (0.25 * bracket * w + saturation) * v
    return a, b, w * m * saturation, saturation


def face(v, s, a, b, vj, sj, aj, bj):
    return (a + aj) * (v - vj) + (b + bj) * (sj - s)


def kernel(
    nt,
    ns,
    nz,
    H,
    R,
    v_h,
    s_h,
    k_h,
    al_h,
    ph_h,
    pond_h,
    sx_h,
    sy_h,
    man_h,
    riv_h,
    code_h,
    out,
    surf,
    v_s,
    s_s,
    k_s,
    al_s,
    ph_s,
    sa,
    sb,
    pond,
    sx,
    sy,
    man,
    riv,
    code,
    c_all,
    c_xp,
    c_xm,
    c_yp,
    c_ym,
    top_stage,
    mid,
    rtop,
    cp_stage,
    cm_stage,
    rcp,
    rcm,
    row_up,
    row_dn,
    rrow_up,
    rrow_dn,
    col_l,
    col_r,
    rcol_l,
    rcol_r,
    pt,
    ft,
    load_sem,
    a_send,
    a_recv,
    b_send,
    b_recv,
    cf_send,
    cf_recv,
    halo_send,
    halo_recv,
    ok_halo,
    ok_rim,
):
    t = lax.axis_index("tile")
    s = lax.axis_index("slab")
    t_prev, t_next = lax.rem(t + nt - 1, nt), lax.rem(t + 1, nt)
    s_prev, s_next = lax.rem(s + ns - 1, ns), lax.rem(s + 1, ns)
    n_y = ns // 4
    y, core = lax.rem(lax.div(s, 2), n_y), lax.rem(s, 2)
    g = lax.div(s, 2 * n_y) * 2 + core

    def slab_at(gg, yy):
        return lax.div(gg, 2) * (2 * n_y) + yy * 2 + lax.rem(gg, 2)

    def place(j):
        return j // 2 % n_y, j // (2 * n_y) * 2 + j % 2

    others_g = [lax.rem(g + d, 4) for d in range(1, 4)]
    others_y = [lax.rem(y + d, n_y) for d in range(1, n_y)]

    half = nt // 2
    late_up, early_up = (t > 0) & (t != half), t == half
    late_down, early_down = t == half - 1, (t < nt - 1) & (t != half - 1)

    inside = pl.ds(1, nz)
    loads = []
    for i, (src, dst) in enumerate(
        [
            (v_h, v_s.at[inside]),
            (s_h, s_s.at[inside]),
            (k_h, k_s),
            (al_h, al_s),
            (pond_h, pond),
            (sx_h, sx),
            (sy_h, sy),
            (man_h, man),
            (riv_h, riv),
            (code_h, code),
            (ph_h, ph_s),
        ]
    ):
        copy = pltpu.make_async_copy(src, dst, load_sem.at[i])
        copy.start()
        loads.append(copy)

    barrier = pltpu.get_barrier_semaphore()

    def greet(tt, ss):
        pl.semaphore_signal(barrier, inc=1, device_id=(tt, ss), device_id_type=MESH)

    for gg in others_g:
        greet(t, slab_at(gg, y))
    for yy in others_y:
        greet(t, slab_at(g, yy))
    greet(t, jnp.where(core == 1, s_next, s_prev))

    def greet_tile(mine, other, s_in, s_late):
        @pl.when(mine)
        def _():
            greet(other, s)

            @pl.when(s == s_in)
            def _():
                greet(other, s_late)

    greet_tile(early_down, t_next, ns - 1, 0)
    greet_tile(early_up, t_prev, 0, ns - 1)

    zero = jnp.zeros((H, W), jnp.float32)
    for ref in (v_s, s_s, sa, sb):
        ref[0] = zero
        ref[nz + 1] = zero

    fields = ((v_s, 1), (s_s, 1), (k_s, 0), (al_s, 0))
    for f, (ref, first) in enumerate(fields):
        loads[f].wait()
        for layer in range(nz):
            k = f * nz + layer
            row_up[k : k + 1, :] = ref[layer + first, 0:1, :]
            row_dn[k : k + 1, :] = ref[layer + first, H - 1 : H, :]

    for j in range(ns):
        lo, hi = max(R * j - 1, 0), min(R * j + R + 1, H)
        at = lo - (R * j - 1)
        yj, gj = place(j)
        top_stage[gj, yj, at : at + hi - lo, :] = v_s[1, lo:hi, :]
    top_stage[0, 0, 0:1, :] = v_s[1, 0:1, :]
    top_stage[3, n_y - 1, R + 1 : R + 2, :] = v_s[1, H - 1 : H, :]

    late = late_up.astype(jnp.int32), late_down.astype(jnp.int32)
    at_first, at_last = (s == 0).astype(jnp.int32), (s == ns - 1).astype(jnp.int32)
    pl.semaphore_wait(
        barrier,
        3 + n_y + late[0] * (1 + at_first) + late[1] * (1 + at_last),
    )

    def send(src, dst, send_sem, recv_sem, tt, ss):
        return pltpu.make_async_remote_copy(
            src_ref=src,
            dst_ref=dst,
            send_sem=send_sem,
            recv_sem=recv_sem,
            device_id=(tt, ss),
            device_id_type=MESH,
        )

    row_copies = [
        send(row_up, rrow_dn, halo_send.at[0], halo_recv.at[0], t_prev, s),
        send(row_dn, rrow_up, halo_send.at[1], halo_recv.at[1], t_next, s),
    ]
    tile_flows = [
        send(cm_stage, rcm, cf_send.at[1], cf_recv.at[1], t_prev, ns - 1),
        send(cp_stage, rcp, cf_send.at[0], cf_recv.at[0], t_next, 0),
    ]
    slab_coefs = [
        send(cm_stage, rcm, cf_send.at[1], cf_recv.at[1], t, s_prev),
        send(cp_stage, rcp, cf_send.at[0], cf_recv.at[0], t, s_next),
    ]
    col_copies = [
        send(col_l, rcol_r, halo_send.at[2], halo_recv.at[2], t, s_prev),
        send(col_r, rcol_l, halo_send.at[3], halo_recv.at[3], t, s_next),
    ]

    first_stage = [
        send(top_stage.at[gg], mid.at[g], a_send.at[d], a_recv.at[g], t, slab_at(gg, y))
        for d, gg in enumerate(others_g)
    ]
    first_arrivals = [
        send(top_stage.at[gg], mid.at[gg], a_send.at[d], a_recv.at[gg], t, slab_at(gg, y))
        for d, gg in enumerate(others_g)
    ]
    second_stage = [
        send(mid.at[:, yy], rtop.at[y], b_send.at[d], b_recv.at[y], t, slab_at(g, yy))
        for d, yy in enumerate(others_y)
    ]
    second_arrivals = [
        send(mid.at[:, yy], rtop.at[yy], b_send.at[d], b_recv.at[yy], t, slab_at(g, yy))
        for d, yy in enumerate(others_y)
    ]

    def late_sends(mine, side, other, s_late):
        @pl.when(mine)
        def _():
            row_copies[side].start()
            pl.semaphore_signal(
                ok_halo.at[1 - side], inc=1, device_id=(other, s), device_id_type=MESH
            )

            @pl.when(s == s_late)
            def _():
                pl.semaphore_signal(
                    ok_rim.at[1 - side],
                    inc=1,
                    device_id=(other, ns - 1 - s_late),
                    device_id_type=MESH,
                )

    late_sends(late_down, 1, t_next, ns - 1)
    late_sends(late_up, 0, t_prev, 0)

    for copy in first_stage:
        copy.start()
    mid[g] = top_stage[g]

    for i in range(4, 10):
        loads[i].wait()
    for j in range(ns):
        cols = slice(j * W, j * W + W)
        conveyance = (5.0 / 3.0) * jnp.exp((2.0 / 3.0) * jnp.log(pond[:, cols])) / man[:, cols]
        along, beside = sx[:, cols], sy[:, cols]
        cx = jnp.where(riv[:, cols] == 1, 0.0, conveyance * (along * lax.rsqrt(along)))
        cy = conveyance * (beside * lax.rsqrt(beside))
        bits = code[:, cols]
        xp = jnp.where((bits & 1) == 1, cx, 0.0)
        xm = cx - xp
        yp = jnp.where(lax.shift_right_logical(bits, 1) == 1, cy, 0.0)
        c_all[j] = cx + cy
        c_xp[j, 0:1, :] = jnp.zeros((1, W), jnp.float32)
        c_xp[j, 1:R, :] = xp[0 : R - 1]
        c_xm[j, 0 : R - 1, :] = xm[1:R]
        c_xm[j, R - 1 : R, :] = jnp.zeros((1, W), jnp.float32)
        c_yp[j] = yp
        c_ym[j] = cy - yp
        cp_stage[j] = xp[R - 1 : R]
        cm_stage[j] = xm[0:1]

    @pl.when(s > 0)
    def _():
        slab_coefs[0].start()

    @pl.when(s < ns - 1)
    def _():
        slab_coefs[1].start()

    lane = lax.broadcasted_iota(jnp.int32, (8, W), 1)
    sub = lax.broadcasted_iota(jnp.int32, (8, W), 0)
    pair = lax.shift_right_logical(lane, 1)
    edges = [jnp.zeros((8, W), jnp.float32) for _ in range(H // 8)]
    for f, (ref, first) in enumerate(fields):
        for layer in range(nz):
            k = f * nz + layer
            here = pair == k
            for c in range(H // 8):
                x = ref[layer + first, c * 8 : c * 8 + 8, :]
                edges[c] = jnp.where(here, pltpu.roll(x, 2 * k + 1, 1), edges[c])
    pt[...] = jnp.concatenate(edges, axis=0).T
    col_l[...] = pt[pl.ds(1, 4 * nz, stride=2), :]
    col_r[...] = pt[pl.ds(0, 4 * nz, stride=2), :]
    for copy in col_copies:
        copy.start()

    loads[10].wait()
    inner_lane = lane < W - 1
    first_row = sub == 0

    def one_layer(layer):
        lp = layer + 1
        before = jnp.maximum(layer - 1, 0)
        for c in range(H // 8):
            rows = slice(c * 8, c * 8 + 8)
            v = v_s[lp, rows, :]
            a, b, sat_deriv, saturation = half_state(
                v, s_s[lp, rows, :], k_s[layer, rows, :], al_s[layer, rows, :]
            )
            sa[lp, rows, :] = a
            sb[lp, rows, :] = b
            out[layer, rows, :] = (
                specific_storage * saturation + ph_s[layer, rows, :] * sat_deriv
            ) * v
        carried = jnp.zeros((8, W), jnp.float32)
        for c in range(H // 8):
            rows = slice(c * 8, c * 8 + 8)
            here = [ref[lp, rows, :] for ref in (v_s, s_s, sa, sb)]
            beside = [pltpu.roll(x, W - 1, 1) for x in here]
            flux = jnp.where(inner_lane, face(*here, *beside), 0.0)
            total = out[layer, rows, :] + flux - pltpu.roll(flux, 1, 1)
            if c < H // 8 - 1:
                after = slice(c * 8 + 1, c * 8 + 9)
                flux = face(*here, *[ref[lp, after, :] for ref in (v_s, s_s, sa, sb)])
            else:
                flux = jnp.where(sub == 7, 0.0, face(*here, *[pltpu.roll(x, 7, 0) for x in here]))
            shifted = pltpu.roll(flux, 1, 0)
            total = total + flux - jnp.where(first_row, carried, shifted)
            carried = shifted
            v, suction, a, b = here
            above = [ref[layer, rows, :] for ref in (v_s, s_s, sa, sb)]
            flux = (a + above[2]) * (above[0] - v) + (b + above[3]) * (suction - above[1] + 1.0)
            out[before, rows, :] = out[before, rows, :] + flux
            out[layer, rows, :] = total - flux

    pl.loop(0, nz // 2)(one_layer)
    for copy in first_arrivals:
        copy.wait_recv()
    for copy in second_stage:
        copy.start()
    rtop[y] = mid[:, y]
    pl.loop(nz // 2, nz)(one_layer)

    for c in range(H // 8):
        rows = slice(c * 8, c * 8 + 8)
        out[nz - 1, rows, :] = (
            out[nz - 1, rows, :]
            + sa[nz, rows, :] * v_s[nz, rows, :]
            + sb[nz, rows, :] * (1.0 - s_s[nz, rows, :])
        )

    def parts(ref):
        return [ref[f * nz : f * nz + nz, :] for f in range(4)]

    def edge_state(raw):
        a, b, _, _ = half_state(*raw)
        return raw[0], raw[1], a, b

    def outside(exists, raw):
        return [jnp.where(exists, x, 0.0) for x in edge_state(raw)]

    def early_rows(mine, side):
        @pl.when(mine)
        def _():
            pl.semaphore_wait(ok_halo.at[side], 1)
            row_copies[side].start()

    def early_flow(mine, side):
        @pl.when(mine)
        def _():
            pl.semaphore_wait(ok_rim.at[side], 1)
            tile_flows[side].start()

    early_rows(early_down, 1)

    for copy in col_copies:
        copy.wait_recv()
    ft[...] = jnp.zeros(ft.shape, jnp.float32)
    ft[pl.ds(1, nz, stride=2), :] = face(
        *edge_state(parts(col_l)), *outside(s > 0, parts(rcol_l))
    )
    ft[pl.ds(0, nz, stride=2), :] = face(
        *edge_state(parts(col_r)), *outside(s < ns - 1, parts(rcol_r))
    )
    turned = ft[...].T
    rim_lane = (lane == 0) | (lane == W - 1)
    for layer in range(nz):
        for c in range(H // 8):
            rows = slice(c * 8, c * 8 + 8)
            x = pltpu.roll(turned[rows], W - (2 * layer + 1), 1)
            out[layer, rows, :] = out[layer, rows, :] + jnp.where(rim_lane, x, 0.0)

    @pl.when(s > 0)
    def _():
        slab_coefs[1].wait_recv()
        for j in range(ns):
            c_xp[j, 0:1, :] = rcp[j]

    @pl.when(s < ns - 1)
    def _():
        slab_coefs[0].wait_recv()
        for j in range(ns):
            c_xm[j, R - 1 : R, :] = rcm[j]

    for copy in second_arrivals:
        copy.wait_recv()

    def top_rows(j, rows):
        yj, gj = place(j)
        return rtop[yj, gj, rows, :]

    @pl.when((s == 0) & (t > 0))
    def _():
        for j in range(ns):
            cm_stage[j] = cm_stage[j] * top_rows(j, slice(1, 2))

    @pl.when((s == ns - 1) & (t < nt - 1))
    def _():
        for j in range(ns):
            cp_stage[j] = cp_stage[j] * top_rows(j, slice(R, R + 1))

    @pl.when(late_up & (s == 0))
    def _():
        tile_flows[0].start()

    @pl.when(late_down & (s == ns - 1))
    def _():
        tile_flows[1].start()

    early_flow(early_down & (s == ns - 1), 1)

    small_lane = lax.broadcasted_iota(jnp.int32, (R, W), 1)
    first, last = small_lane == 0, small_lane == W - 1
    nil = jnp.zeros((R, W), jnp.float32)
    prev_plus = nil
    tops = [top_rows(j, slice(1, R + 1)) for j in range(ns)]
    minus = [pltpu.roll(c_ym[j] * tops[j], W - 1, 1) for j in range(ns)] + [nil]
    for j in range(ns):
        plus = pltpu.roll(c_yp[j] * tops[j], 1, 1)
        surf[:, j * W : j * W + W] = (
            c_all[j] * tops[j]
            - c_xp[j] * top_rows(j, slice(0, R))
            - c_xm[j] * top_rows(j, slice(2, R + 2))
            - jnp.where(first, prev_plus, plus)
            - jnp.where(last, minus[j + 1], minus[j])
        )
        prev_plus = plus

    early_rows(early_up, 0)
    early_flow(early_up & (s == 0), 0)

    def add_rows(exists, copy, own, theirs, row):
        @pl.when(exists)
        def _():
            copy.wait_recv()
            flux = face(*edge_state(parts(own)), *edge_state(parts(theirs)))
            for layer in range(nz):
                out[layer, row : row + 1, :] = (
                    out[layer, row : row + 1, :] + flux[layer : layer + 1]
                )

        @pl.when(jnp.logical_not(exists))
        def _():
            v, suction, a, b = edge_state(parts(own))
            flux = a * v - b * suction
            for layer in range(nz):
                out[layer, row : row + 1, :] = (
                    out[layer, row : row + 1, :] + flux[layer : layer + 1]
                )

    add_rows(t < nt - 1, row_copies[0], row_dn, rrow_dn, H - 1)
    add_rows(t > 0, row_copies[1], row_up, rrow_up, 0)

    def add_flow(exists, copy, arrived, row):
        @pl.when(exists)
        def _():
            copy.wait_recv()
            for j in range(ns):
                cols = slice(j * W, j * W + W)
                surf[row : row + 1, cols] = surf[row : row + 1, cols] - arrived[j]

    add_flow((t < nt - 1) & (s == ns - 1), tile_flows[0], rcm, R - 1)
    add_flow((t > 0) & (s == 0), tile_flows[1], rcp, 0)

    for copy in col_copies:
        copy.wait_send()
    for side, exists in ((0, t > 0), (1, t < nt - 1)):

        @pl.when(exists)
        def _(side=side):
            row_copies[side].wait_send()

    @pl.when((s > 0) | (t > 0))
    def _():
        slab_coefs[0].wait_send()

    @pl.when((s < ns - 1) | (t < nt - 1))
    def _():
        slab_coefs[1].wait_send()

    for copy in first_stage + second_stage:
        copy.wait_send()


def per_device(nt, ns, *args):
    nz, H, _ = args[0].shape
    R = args[5].shape[0]
    f32 = jnp.float32
    vm = pltpu.VMEM
    dma = pltpu.SemaphoreType.DMA
    anywhere = pl.BlockSpec(memory_space=pl.ANY)
    return pl.pallas_call(
        functools.partial(kernel, nt, ns, nz, H, R),
        out_shape=(
            vm((nz, H, W), f32),
            vm((R, ns * W), f32),
        ),
        in_specs=[anywhere] * 11,
        out_specs=(pl.BlockSpec(memory_space=pltpu.VMEM),) * 2,
        scratch_shapes=[
            vm((nz + 2, H, W), f32),
            vm((nz + 2, H, W), f32),
            vm((nz, H, W), f32),
            vm((nz, H, W), f32),
            vm((nz, H, W), f32),
            vm((nz + 2, H, W), f32),
            vm((nz + 2, H, W), f32),
            vm((R, ns * W), f32),
            vm((R, ns * W), f32),
            vm((R, ns * W), f32),
            vm((R, ns * W), f32),
            vm((R, ns * W), jnp.int32),
            vm((R, ns * W), jnp.int32),
            vm((ns, R, W), f32),
            vm((ns, R, W), f32),
            vm((ns, R, W), f32),
            vm((ns, R, W), f32),
            vm((ns, R, W), f32),
            vm((4, ns // 4, R + 2, W), f32),
            vm((4, ns // 4, R + 2, W), f32),
            vm((ns // 4, 4, R + 2, W), f32),
            vm((ns, 1, W), f32),
            vm((ns, 1, W), f32),
            vm((ns, 1, W), f32),
            vm((ns, 1, W), f32),
            vm((4 * nz, W), f32),
            vm((4 * nz, W), f32),
            vm((4 * nz, W), f32),
            vm((4 * nz, W), f32),
            vm((4 * nz, H), f32),
            vm((4 * nz, H), f32),
            vm((4 * nz, H), f32),
            vm((4 * nz, H), f32),
            vm((W, H), f32),
            vm((W, H), f32),
            dma((11,)),
            dma((4,)),
            dma((4,)),
            dma((ns // 4,)),
            dma((ns // 4,)),
            dma((2,)),
            dma((2,)),
            dma((4,)),
            dma((4,)),
            pltpu.SemaphoreType.REGULAR((2,)),
            pltpu.SemaphoreType.REGULAR((2,)),
        ],
        compiler_params=pltpu.CompilerParams(
            collective_id=0, has_side_effects=True, vmem_limit_bytes=56 * 1024 * 1024
        ),
    )(*args)


def solution(mesh):
    cells = P(None, "tile", "slab")
    surface = P(("tile", "slab"), None)
    return jax.shard_map(
        functools.partial(per_device, mesh.shape["tile"], mesh.shape["slab"]),
        mesh=mesh,
        in_specs=(cells,) * 5 + (surface,) * 6,
        out_specs=(cells, surface),
        check_vma=False,
    )
```

time: 31.4 us -> 31.8 us (1.013)
  the two profiles are of different devices: /device:TPU:1 before, /device:TPU:2 now
where the time goes in v2:
time: 31.8 us; the launch traced here: 31.6 us
  Pallas kernels  29.5 us (93%)
  local copies, waits for them, and re-layouts  1.47 us (5%)
  between operations  0.64 us (2%)
    pallas_call x1, Pallas kernels, per_device(): pl.pallas_call(functools.partial(kernel, nt, ns, nz, H, R), out_shape=(vm...  29.5 us
    unnamed x2, local copies, waits for them, and re-layouts  1.47 us

profile of v2, /device:TPU:2, one launch (start us, length us, event | category | flops | bytes accessed | tf_op | source)
XLA Modules:
  0.0 31.6 jit_solution(13153144571167440039)
XLA Ops:
  0.6 29.5 %shard_map.122 = (f32[10,128,128]{2,1,0:T(8,128)S(1)}, f32[4,4096]{1,0:T(4,128)S(1)}) custom-call(f32[10,128,128]{2,1,0:T(8,128)} %v_h.1, f32[10,128,128]{2,1,0:T(8,128)} %s_h.1, f32[10,128,128]{2,1,0:T(8,128)} %k_h.1, f32[10,128,128]{2,1,0:T(8,128)} %al_h.1, f32[10,128,128]{2,1,0:T(8,128)} %ph_h.1, f32[4,4096]{1,0:T(4,128)} %pond_h.1, f32[4,4096]{1,0:T(4,128)} %sx_h.1, ...), custom_call_target="tpu_custom_call" | custom-call | tf_op jit(solution)/shard_map/pallas_call | solution.py:525
  30.1 0.8 %copy.15 = f32[10,128,128]{2,1,0:T(8,128)} copy(f32[10,128,128]{2,1,0:T(8,128)S(1)} %get-tuple-element.2) | data formatting | bytes 1310720
  31.0 0.6 %copy.16 = f32[4,4096]{1,0:T(4,128)} copy(f32[4,4096]{1,0:T(4,128)S(1)} %get-tuple-element.3) | data formatting | bytes 131072

commit v3 on v2

v3 whole, which is shorter than its diff:
```python
import functools

import jax
import jax.numpy as jnp
from jax import lax
from jax.experimental import pallas as pl
from jax.experimental.pallas import tpu as pltpu
from jax.sharding import PartitionSpec as P

MESH = pl.DeviceIdType.MESH
W = 128
specific_storage = 0.01


def relative(suction, vg_alpha):
    w = vg_alpha * suction
    saturation = lax.rsqrt(1.0 + w * w)
    quarter = saturation * lax.rsqrt(saturation)
    bracket = 1.0 - w * saturation
    return w, saturation, quarter, bracket


def half_state(v, suction, conductivity, vg_alpha):
    w, saturation, quarter, bracket = relative(suction, vg_alpha)
    kb = conductivity * quarter * bracket
    m = vg_alpha * saturation * saturation
    a = 0.5 * kb * bracket
    b = kb * m * (0.25 * bracket * w + saturation) * v
    return a, b, w * m * saturation, saturation


def face(v, s, a, b, vj, sj, aj, bj):
    return (a + aj) * (v - vj) + (b + bj) * (sj - s)


def kernel(
    nt,
    ns,
    nz,
    H,
    R,
    v_h,
    s_h,
    k_h,
    al_h,
    ph_h,
    pond_h,
    sx_h,
    sy_h,
    man_h,
    riv_h,
    code_h,
    out,
    surf,
    v_s,
    s_s,
    k_s,
    al_s,
    ph_s,
    sa,
    sb,
    pond,
    sx,
    sy,
    man,
    riv,
    code,
    c_all,
    c_xp,
    c_xm,
    c_yp,
    c_ym,
    top_stage,
    rtop,
    rim_stage,
    rim,
    cp_stage,
    cm_stage,
    rcp,
    rcm,
    row_up,
    row_dn,
    rrow_up,
    rrow_dn,
    col_l,
    col_r,
    rcol_l,
    rcol_r,
    pt,
    ft,
    load_sem,
    top_send,
    top_recv,
    rim_send,
    rim_recv,
    cf_send,
    cf_recv,
    halo_send,
    halo_recv,
    ok_halo,
    ok_rim,
):
    t = lax.axis_index("tile")
    s = lax.axis_index("slab")
    t_prev, t_next = lax.rem(t + nt - 1, nt), lax.rem(t + 1, nt)
    s_prev, s_next = lax.rem(s + ns - 1, ns), lax.rem(s + 1, ns)
    half = nt // 2
    early_up = (t == half) | (t == 1)
    late_up = (t > 0) & jnp.logical_not(early_up)
    late_down = (t == half - 1) | (t == 0)
    early_down = (t < nt - 1) & jnp.logical_not(late_down)

    inside = pl.ds(1, nz)
    loads = []
    for i, (src, dst) in enumerate(
        [
            (v_h, v_s.at[inside]),
            (s_h, s_s.at[inside]),
            (k_h, k_s),
            (al_h, al_s),
            (pond_h, pond),
            (sx_h, sx),
            (sy_h, sy),
            (man_h, man),
            (riv_h, riv),
            (code_h, code),
            (ph_h, ph_s),
        ]
    ):
        copy = pltpu.make_async_copy(src, dst, load_sem.at[i])
        loads.append(copy)
    loads[0].start()

    barrier = pltpu.get_barrier_semaphore()

    def greet(tt, ss):
        pl.semaphore_signal(barrier, inc=1, device_id=(tt, ss), device_id_type=MESH)

    for d in range(ns // 2):
        for peer in {ns // 2 - d, ns // 2 + d} - {ns}:
            greet(t, lax.rem(s + peer, ns))

    def greet_tile(mine, other, s_in):
        @pl.when(mine)
        def _():
            @pl.when(s == s_in)
            def _():
                @pl.loop(0, ns)
                def _(j):
                    greet(other, j)

            @pl.when(s != s_in)
            def _():
                greet(other, s)

    greet_tile(early_down, t_next, ns - 1)
    greet_tile(early_up, t_prev, 0)
    for copy in loads[1:]:
        copy.start()

    loads[0].wait()
    rim_stage[0] = v_s[1, 0:1, :]
    rim_stage[1] = v_s[1, H - 1 : H, :]
    for j in range(ns):
        lo, hi = max(R * j - 1, 0), min(R * j + R + 1, H)
        at = lo - (R * j - 1)
        top_stage[j, at : at + hi - lo, :] = v_s[1, lo:hi, :]
    top_stage[0, 0:1, :] = v_s[1, 0:1, :]
    top_stage[ns - 1, R + 1 : R + 2, :] = v_s[1, H - 1 : H, :]

    fields = ((v_s, 1), (s_s, 1), (k_s, 0), (al_s, 0))

    lane = lax.broadcasted_iota(jnp.int32, (8, W), 1)
    sub = lax.broadcasted_iota(jnp.int32, (8, W), 0)
    pair = lax.shift_right_logical(lane, 1)

    def local_rows():
        zero = jnp.zeros((H, W), jnp.float32)
        for ref in (v_s, s_s, sa, sb):
            ref[0] = zero
            ref[nz + 1] = zero

        for f, (ref, first) in enumerate(fields):
            if f > 0:
                loads[f].wait()
            for layer in range(nz):
                k = f * nz + layer
                row_up[k : k + 1, :] = ref[layer + first, 0:1, :]
                row_dn[k : k + 1, :] = ref[layer + first, H - 1 : H, :]

    def local_coefficients():
        for i in range(4, 10):
            loads[i].wait()
        for j in range(ns):
            cols = slice(j * W, j * W + W)
            conveyance = (5.0 / 3.0) * jnp.exp((2.0 / 3.0) * jnp.log(pond[:, cols])) / man[:, cols]
            along, beside = sx[:, cols], sy[:, cols]
            cx = jnp.where(riv[:, cols] == 1, 0.0, conveyance * (along * lax.rsqrt(along)))
            cy = conveyance * (beside * lax.rsqrt(beside))
            bits = code[:, cols]
            xp = jnp.where((bits & 1) == 1, cx, 0.0)
            xm = cx - xp
            yp = jnp.where(lax.shift_right_logical(bits, 1) == 1, cy, 0.0)
            c_all[j] = cx + cy
            c_xp[j, 0:1, :] = jnp.zeros((1, W), jnp.float32)
            c_xp[j, 1:R, :] = xp[0 : R - 1]
            c_xm[j, 0 : R - 1, :] = xm[1:R]
            c_xm[j, R - 1 : R, :] = jnp.zeros((1, W), jnp.float32)
            c_yp[j] = yp
            c_ym[j] = cy - yp
            cp_stage[j : j + 1, :] = xp[R - 1 : R]
            cm_stage[j : j + 1, :] = xm[0:1]

    def local_columns():
        edges = [jnp.zeros((8, W), jnp.float32) for _ in range(H // 8)]
        for f, (ref, first) in enumerate(fields):
            for layer in range(nz):
                k = f * nz + layer
                here = pair == k
                for c in range(H // 8):
                    x = ref[layer + first, c * 8 : c * 8 + 8, :]
                    edges[c] = jnp.where(here, pltpu.roll(x, 2 * k + 1, 1), edges[c])
        pt[...] = jnp.concatenate(edges, axis=0).T
        col_l[...] = pt[pl.ds(1, 4 * nz, stride=2), :]
        col_r[...] = pt[pl.ds(0, 4 * nz, stride=2), :]
        loads[10].wait()

    inner_lane = lane < W - 1
    first_row = sub == 0

    def one_layer(layer):
        lp = layer + 1
        before = jnp.maximum(layer - 1, 0)
        for c in range(H // 8):
            rows = slice(c * 8, c * 8 + 8)
            v = v_s[lp, rows, :]
            a, b, sat_deriv, saturation = half_state(
                v, s_s[lp, rows, :], k_s[layer, rows, :], al_s[layer, rows, :]
            )
            sa[lp, rows, :] = a
            sb[lp, rows, :] = b
            out[layer, rows, :] = (
                specific_storage * saturation + ph_s[layer, rows, :] * sat_deriv
            ) * v
        carried = jnp.zeros((8, W), jnp.float32)
        for c in range(H // 8):
            rows = slice(c * 8, c * 8 + 8)
            here = [ref[lp, rows, :] for ref in (v_s, s_s, sa, sb)]
            beside = [pltpu.roll(x, W - 1, 1) for x in here]
            flux = jnp.where(inner_lane, face(*here, *beside), 0.0)
            total = out[layer, rows, :] + flux - pltpu.roll(flux, 1, 1)
            if c < H // 8 - 1:
                after = slice(c * 8 + 1, c * 8 + 9)
                flux = face(*here, *[ref[lp, after, :] for ref in (v_s, s_s, sa, sb)])
            else:
                flux = jnp.where(sub == 7, 0.0, face(*here, *[pltpu.roll(x, 7, 0) for x in here]))
            shifted = pltpu.roll(flux, 1, 0)
            total = total + flux - jnp.where(first_row, carried, shifted)
            carried = shifted
            v, suction, a, b = here
            above = [ref[layer, rows, :] for ref in (v_s, s_s, sa, sb)]
            flux = (a + above[2]) * (above[0] - v) + (b + above[3]) * (suction - above[1] + 1.0)
            out[before, rows, :] = out[before, rows, :] + flux
            out[layer, rows, :] = total - flux

    patient = (t == 0) & (s > 0)
    prepared = (t == 0) | (t == half - 1)
    pl.when(prepared)(local_rows)
    pl.when(prepared)(local_coefficients)
    pl.when(patient)(local_columns)
    pl.loop(0, jnp.where(patient, nz, 0))(one_layer)

    late = late_up.astype(jnp.int32), late_down.astype(jnp.int32)
    at_first, at_last = (s == 0).astype(jnp.int32), (s == ns - 1).astype(jnp.int32)
    pl.semaphore_wait(
        barrier,
        ns - 1 + late[0] * (2 - at_last) + late[1] * (2 - at_first),
    )

    def send(src, dst, send_sem, recv_sem, tt, ss):
        return pltpu.make_async_remote_copy(
            src_ref=src,
            dst_ref=dst,
            send_sem=send_sem,
            recv_sem=recv_sem,
            device_id=(tt, ss),
            device_id_type=MESH,
        )

    row_copies = [
        send(row_up, rrow_dn, halo_send.at[0], halo_recv.at[0], t_prev, s),
        send(row_dn, rrow_up, halo_send.at[1], halo_recv.at[1], t_next, s),
    ]
    rims = [
        send(rim_stage.at[0], rim.at[s], rim_send.at[0], rim_recv.at[0], t_prev, ns - 1),
        send(rim_stage.at[1], rim.at[s], rim_send.at[1], rim_recv.at[0], t_next, 0),
    ]
    tile_flows = [
        send(cm_stage, rcm, cf_send.at[1], cf_recv.at[1], t_prev, ns - 1),
        send(cp_stage, rcp, cf_send.at[0], cf_recv.at[0], t_next, 0),
    ]
    slab_coefs = [
        send(cm_stage, rcm, cf_send.at[1], cf_recv.at[1], t, s_prev),
        send(cp_stage, rcp, cf_send.at[0], cf_recv.at[0], t, s_next),
    ]
    col_copies = [
        send(col_l, rcol_r, halo_send.at[2], halo_recv.at[2], t, s_prev),
        send(col_r, rcol_l, halo_send.at[3], halo_recv.at[3], t, s_next),
    ]

    peers = [lax.rem(s + d, ns) for d in range(1, ns)]
    tops = [
        send(top_stage.at[peer], rtop.at[s], top_send.at[0], top_recv.at[0], t, peer)
        for peer in peers
    ]
    all_tops = send(
        top_stage.at[1:], rtop.at[1:], top_send.at[0], top_recv.at[0], t, s_next
    )
    all_rims = send(rim, rim, rim_send.at[0], rim_recv.at[0], t_next, 0)

    def late_sends(mine, side, other, s_late):
        @pl.when(mine)
        def _():
            row_copies[side].start()
            pl.semaphore_signal(
                ok_halo.at[1 - side], inc=1, device_id=(other, s), device_id_type=MESH
            )

            @pl.when(s == s_late)
            def _():
                pl.semaphore_signal(
                    ok_rim.at[1 - side],
                    inc=1,
                    device_id=(other, ns - 1 - s_late),
                    device_id_type=MESH,
                )

    for side, exists in ((1, late_down), (0, late_up)):
        pl.when(exists)(rims[side].start)

    @pl.when(late_down & (s == ns - 1))
    def _():
        tile_flows[1].start()

    late_sends(late_down, 1, t_next, ns - 1)
    for copy in tops:
        copy.start()
    rtop[s] = top_stage[s]
    unprepared = jnp.logical_not(prepared)
    pl.when(unprepared)(local_rows)
    late_sends(late_up, 0, t_prev, 0)
    pl.when(unprepared)(local_coefficients)

    @pl.when(late_up & (s == 0))
    def _():
        tile_flows[0].start()

    pl.when(jnp.logical_not(patient))(local_columns)


    @pl.when(s > 0)
    def _():
        slab_coefs[0].start()

    @pl.when(s < ns - 1)
    def _():
        slab_coefs[1].start()

    for copy in col_copies:
        copy.start()

    def early_rows(mine, side):
        @pl.when(mine)
        def _():
            pl.semaphore_wait(ok_halo.at[side], 1)
            row_copies[side].start()

    def early_flow(mine, side):
        @pl.when(mine)
        def _():
            pl.semaphore_wait(ok_rim.at[side], 1)
            tile_flows[side].start()

    def top_rows(j, rows):
        return rtop[j, rows, :]

    flowing = early_down & (s == ns - 1)
    middle = jnp.where(flowing, nz // 2, nz)
    pl.loop(jnp.where(patient, nz, 0), middle)(one_layer)

    @pl.when(flowing)
    def _():
        all_tops.wait_recv()
        for j in range(ns):
            cp_stage[j : j + 1, :] = cp_stage[j : j + 1, :] * top_rows(j, slice(R, R + 1))

    early_flow(flowing, 1)
    pl.loop(middle, nz)(one_layer)

    for c in range(H // 8):
        rows = slice(c * 8, c * 8 + 8)
        out[nz - 1, rows, :] = (
            out[nz - 1, rows, :]
            + sa[nz, rows, :] * v_s[nz, rows, :]
            + sb[nz, rows, :] * (1.0 - s_s[nz, rows, :])
        )

    def parts(ref):
        return [ref[f * nz : f * nz + nz, :] for f in range(4)]

    def edge_state(raw):
        a, b, _, _ = half_state(*raw)
        return raw[0], raw[1], a, b

    def outside(exists, raw):
        return [jnp.where(exists, x, 0.0) for x in edge_state(raw)]

    early_rows(early_down, 1)
    if half != 1:
        early_rows(t == 1, 0)

    pl.when(jnp.logical_not(flowing))(all_tops.wait_recv)

    @pl.when(early_up & (s == 0))
    def _():
        for j in range(ns):
            cm_stage[j : j + 1, :] = cm_stage[j : j + 1, :] * top_rows(j, slice(1, 2))

    for copy in col_copies:
        copy.wait_recv()
    ft[...] = jnp.zeros(ft.shape, jnp.float32)
    ft[pl.ds(1, nz, stride=2), :] = face(
        *edge_state(parts(col_l)), *outside(s > 0, parts(rcol_l))
    )
    ft[pl.ds(0, nz, stride=2), :] = face(
        *edge_state(parts(col_r)), *outside(s < ns - 1, parts(rcol_r))
    )
    turned = ft[...].T
    rim_lane = (lane == 0) | (lane == W - 1)
    for layer in range(nz):
        for c in range(H // 8):
            rows = slice(c * 8, c * 8 + 8)
            x = pltpu.roll(turned[rows], W - (2 * layer + 1), 1)
            out[layer, rows, :] = out[layer, rows, :] + jnp.where(rim_lane, x, 0.0)

    @pl.when(s > 0)
    def _():
        slab_coefs[1].wait_recv()
        for j in range(ns):
            c_xp[j, 0:1, :] = rcp[j : j + 1, :]

    @pl.when(s < ns - 1)
    def _():
        slab_coefs[0].wait_recv()
        for j in range(ns):
            c_xm[j, R - 1 : R, :] = rcm[j : j + 1, :]

    small_lane = lax.broadcasted_iota(jnp.int32, (R, W), 1)
    first, last = small_lane == 0, small_lane == W - 1
    nil = jnp.zeros((R, W), jnp.float32)
    prev_plus = nil
    own = [top_rows(j, slice(1, R + 1)) for j in range(ns)]
    minus = [pltpu.roll(c_ym[j] * own[j], W - 1, 1) for j in range(ns)] + [nil]
    for j in range(ns):
        plus = pltpu.roll(c_yp[j] * own[j], 1, 1)
        surf[:, j * W : j * W + W] = (
            c_all[j] * own[j]
            - c_xp[j] * top_rows(j, slice(0, R))
            - c_xm[j] * top_rows(j, slice(2, R + 2))
            - jnp.where(first, prev_plus, plus)
            - jnp.where(last, minus[j + 1], minus[j])
        )
        prev_plus = plus

    early_rows(t == half, 0)
    early_flow(early_up & (s == 0), 0)

    def add_rows(exists, copy, own, theirs, row):
        @pl.when(exists)
        def _():
            copy.wait_recv()
            flux = face(*edge_state(parts(own)), *edge_state(parts(theirs)))
            for layer in range(nz):
                out[layer, row : row + 1, :] = (
                    out[layer, row : row + 1, :] + flux[layer : layer + 1]
                )

        @pl.when(jnp.logical_not(exists))
        def _():
            v, suction, a, b = edge_state(parts(own))
            flux = a * v - b * suction
            for layer in range(nz):
                out[layer, row : row + 1, :] = (
                    out[layer, row : row + 1, :] + flux[layer : layer + 1]
                )

    add_rows(t < nt - 1, row_copies[0], row_dn, rrow_dn, H - 1)
    add_rows(t > 0, row_copies[1], row_up, rrow_up, 0)

    def add_flow(early, late, copy, arrived, row):
        @pl.when(late)
        def _():
            copy.wait_recv()
            for j in range(ns):
                cols = slice(j * W, j * W + W)
                surf[row : row + 1, cols] = surf[row : row + 1, cols] - arrived[j : j + 1, :]

        @pl.when(early)
        def _():
            copy.wait_recv()

            all_rims.wait_recv()
            for j in range(ns):
                cols = slice(j * W, j * W + W)
                surf[row : row + 1, cols] = surf[row : row + 1, cols] - arrived[j : j + 1, :] * rim[j]

    at_end, at_start = s == ns - 1, s == 0
    add_flow(early_down & at_end, late_down & at_end, tile_flows[0], rcm, R - 1)
    add_flow(early_up & at_start, late_up & at_start, tile_flows[1], rcp, 0)

    for copy in col_copies:
        copy.wait_send()
    for side, exists in ((0, t > 0), (1, t < nt - 1)):

        @pl.when(exists)
        def _(side=side):
            row_copies[side].wait_send()

    for side, exists in ((0, late_up), (1, late_down)):

        @pl.when(exists)
        def _(side=side):
            rims[side].wait_send()

    @pl.when((s > 0) | (t > 0))
    def _():
        slab_coefs[0].wait_send()

    @pl.when((s < ns - 1) | (t < nt - 1))
    def _():
        slab_coefs[1].wait_send()

    all_tops.wait_send()


def per_device(nt, ns, *args):
    nz, H, _ = args[0].shape
    R = args[5].shape[0]
    f32 = jnp.float32
    vm = pltpu.VMEM
    dma = pltpu.SemaphoreType.DMA
    anywhere = pl.BlockSpec(memory_space=pl.ANY)
    return pl.pallas_call(
        functools.partial(kernel, nt, ns, nz, H, R),
        out_shape=(
            vm((nz, H, W), f32),
            vm((R, ns * W), f32),
        ),
        in_specs=[anywhere] * 11,
        out_specs=(pl.BlockSpec(memory_space=pltpu.VMEM),) * 2,
        scratch_shapes=[
            vm((nz + 2, H, W), f32),
            vm((nz + 2, H, W), f32),
            vm((nz, H, W), f32),
            vm((nz, H, W), f32),
            vm((nz, H, W), f32),
            vm((nz + 2, H, W), f32),
            vm((nz + 2, H, W), f32),
            vm((R, ns * W), f32),
            vm((R, ns * W), f32),
            vm((R, ns * W), f32),
            vm((R, ns * W), f32),
            vm((R, ns * W), jnp.int32),
            vm((R, ns * W), jnp.int32),
            vm((ns, R, W), f32),
            vm((ns, R, W), f32),
            vm((ns, R, W), f32),
            vm((ns, R, W), f32),
            vm((ns, R, W), f32),
            vm((ns, R + 2, W), f32),
            vm((ns, R + 2, W), f32),
            vm((2, 1, W), f32),
            vm((ns, 1, W), f32),
            vm((ns, W), f32),
            vm((ns, W), f32),
            vm((ns, W), f32),
            vm((ns, W), f32),
            vm((4 * nz, W), f32),
            vm((4 * nz, W), f32),
            vm((4 * nz, W), f32),
            vm((4 * nz, W), f32),
            vm((4 * nz, H), f32),
            vm((4 * nz, H), f32),
            vm((4 * nz, H), f32),
            vm((4 * nz, H), f32),
            vm((W, H), f32),
            vm((W, H), f32),
            dma((11,)),
            dma((1,)),
            dma((1,)),
            dma((2,)),
            dma((1,)),
            dma((2,)),
            dma((2,)),
            dma((4,)),
            dma((4,)),
            pltpu.SemaphoreType.REGULAR((2,)),
            pltpu.SemaphoreType.REGULAR((2,)),
        ],
        compiler_params=pltpu.CompilerParams(
            collective_id=0, has_side_effects=True, vmem_limit_bytes=56 * 1024 * 1024
        ),
    )(*args)


def solution(mesh):
    cells = P(None, "tile", "slab")
    surface = P(("tile", "slab"), None)
    return jax.shard_map(
        functools.partial(per_device, mesh.shape["tile"], mesh.shape["slab"]),
        mesh=mesh,
        in_specs=(cells,) * 5 + (surface,) * 6,
        out_specs=(cells, surface),
        check_vma=False,
    )
```

time: 31.8 us -> 26.3 us (0.83)
  Pallas kernels: 29.5 us -> 24 us
    pallas_call x1, Pallas kernels: 29.5 us -> 24 us  [per_device(): pl.pallas_call(functools.partial(kernel, nt, ns, nz, H, R), out_shape=(vm...]
where the time goes in v3:
time: 26.3 us; the launch traced here: 26.1 us
  Pallas kernels  24 us (91%)
  local copies, waits for them, and re-layouts  1.47 us (6%)
  between operations  0.64 us (2%)
    pallas_call x1, Pallas kernels, per_device(): pl.pallas_call(functools.partial(kernel, nt, ns, nz, H, R), out_shape=(vm...  24 us
    unnamed x2, local copies, waits for them, and re-layouts  1.47 us

profile of v3, /device:TPU:2, one launch (start us, length us, event | category | flops | bytes accessed | tf_op | source)
XLA Modules:
  0.0 26.1 jit_solution(14688146543304143603)
XLA Ops:
  0.6 24.0 %shard_map.122 = (f32[10,128,128]{2,1,0:T(8,128)S(1)}, f32[4,4096]{1,0:T(4,128)S(1)}) custom-call(f32[10,128,128]{2,1,0:T(8,128)} %v_h.1, f32[10,128,128]{2,1,0:T(8,128)} %s_h.1, f32[10,128,128]{2,1,0:T(8,128)} %k_h.1, f32[10,128,128]{2,1,0:T(8,128)} %al_h.1, f32[10,128,128]{2,1,0:T(8,128)} %ph_h.1, f32[4,4096]{1,0:T(4,128)} %pond_h.1, f32[4,4096]{1,0:T(4,128)} %sx_h.1, ...), custom_call_target="tpu_custom_call" | custom-call | tf_op jit(solution)/shard_map/pallas_call | solution.py:553
  24.7 0.8 %copy.15 = f32[10,128,128]{2,1,0:T(8,128)} copy(f32[10,128,128]{2,1,0:T(8,128)S(1)} %get-tuple-element.2) | data formatting | bytes 1310720
  25.5 0.6 %copy.16 = f32[4,4096]{1,0:T(4,128)} copy(f32[4,4096]{1,0:T(4,128)S(1)} %get-tuple-element.3) | data formatting | bytes 131072

commit v4 on v3

--- a/solution.py
+++ b/solution.py
@@ -99,15 +99,16 @@
     halo_recv,
     ok_halo,
     ok_rim,
+    ok_slab,
 ):
     t = lax.axis_index("tile")
     s = lax.axis_index("slab")
     t_prev, t_next = lax.rem(t + nt - 1, nt), lax.rem(t + 1, nt)
     s_prev, s_next = lax.rem(s + ns - 1, ns), lax.rem(s + 1, ns)
     half = nt // 2
-    early_up = (t == half) | (t == 1)
+    early_up = (t == half) | (t == 1) | ((t == half - 1) & (t > 0))
     late_up = (t > 0) & jnp.logical_not(early_up)
-    late_down = (t == half - 1) | (t == 0)
+    late_down = (t == half - 1) | (t == half - 2) | (t == 0)
     early_down = (t < nt - 1) & jnp.logical_not(late_down)
 
     inside = pl.ds(1, nz)
@@ -136,9 +137,19 @@
     def greet(tt, ss):
         pl.semaphore_signal(barrier, inc=1, device_id=(tt, ss), device_id_type=MESH)
 
-    for d in range(ns // 2):
-        for peer in {ns // 2 - d, ns // 2 + d} - {ns}:
-            greet(t, lax.rem(s + peer, ns))
+    n_y = ns // 4
+    ranked = t == half - 1
+    n_below = jnp.where(ranked, s, ns - 1)
+
+    def is_above(peer):
+        return ranked & (peer > s)
+
+    def wrapped(peer):
+        return jnp.where(peer >= ns, peer - ns, peer)
+
+    @pl.loop(s + 1, jnp.where(ranked, ns, s + ns))
+    def _(peer):
+        greet(t, wrapped(peer))
 
     def greet_tile(mine, other, s_in):
         @pl.when(mine)
@@ -264,7 +275,10 @@
             out[layer, rows, :] = total - flux
 
     patient = (t == 0) & (s > 0)
-    prepared = (t == 0) | (t == half - 1)
+    y = lax.rem(lax.div(s, 2), n_y)
+    last_started = (s >= ns // 2) & (y >= n_y // 2 - 1) & (y < n_y - 2)
+    prepared = patient | ((t == half - 1) & (s > 0) & jnp.logical_not(last_started))
+    prepared = prepared | (late_down & (s == ns - 1))
     pl.when(prepared)(local_rows)
     pl.when(prepared)(local_coefficients)
     pl.when(patient)(local_columns)
@@ -274,7 +288,7 @@
     at_first, at_last = (s == 0).astype(jnp.int32), (s == ns - 1).astype(jnp.int32)
     pl.semaphore_wait(
         barrier,
-        ns - 1 + late[0] * (2 - at_last) + late[1] * (2 - at_first),
+        n_below + late[0] * (2 - at_last) + late[1] * (2 - at_first),
     )
 
     def send(src, dst, send_sem, recv_sem, tt, ss):
@@ -308,11 +322,11 @@
         send(col_r, rcol_l, halo_send.at[3], halo_recv.at[3], t, s_next),
     ]
 
-    peers = [lax.rem(s + d, ns) for d in range(1, ns)]
-    tops = [
-        send(top_stage.at[peer], rtop.at[s], top_send.at[0], top_recv.at[0], t, peer)
-        for peer in peers
-    ]
+    def top_copy(peer):
+        return send(
+            top_stage.at[peer], rtop.at[s], top_send.at[0], top_recv.at[0], t, peer
+        )
+
     all_tops = send(
         top_stage.at[1:], rtop.at[1:], top_send.at[0], top_recv.at[0], t, s_next
     )
@@ -342,12 +356,20 @@
     def _():
         tile_flows[1].start()
 
-    late_sends(late_down, 1, t_next, ns - 1)
-    for copy in tops:
-        copy.start()
+    late_sends(late_down & prepared, 1, t_next, ns - 1)
+
+    @pl.loop(jnp.where(ranked, 0, s + 1), jnp.where(ranked, s, s + ns))
+    def _(peer):
+        top_copy(wrapped(peer)).start()
+
+    @pl.loop(0, jnp.where(ranked, s, 0))
+    def _(peer):
+        pl.semaphore_signal(ok_slab, inc=1, device_id=(t, peer), device_id_type=MESH)
+
     rtop[s] = top_stage[s]
     unprepared = jnp.logical_not(prepared)
     pl.when(unprepared)(local_rows)
+    late_sends(late_down & unprepared, 1, t_next, ns - 1)
     late_sends(late_up, 0, t_prev, 0)
     pl.when(unprepared)(local_coefficients)
 
@@ -358,16 +380,14 @@
     pl.when(jnp.logical_not(patient))(local_columns)
 
 
-    @pl.when(s > 0)
-    def _():
-        slab_coefs[0].start()
-
-    @pl.when(s < ns - 1)
-    def _():
-        slab_coefs[1].start()
-
-    for copy in col_copies:
-        copy.start()
+    near = [
+        (slab_coefs[0], s_prev, s > 0),
+        (slab_coefs[1], s_next, s < ns - 1),
+        (col_copies[0], s_prev, s >= 0),
+        (col_copies[1], s_next, s >= 0),
+    ]
+    for copy, peer, exists in near:
+        pl.when(exists & jnp.logical_not(is_above(peer)))(copy.start)
 
     def early_rows(mine, side):
         @pl.when(mine)
@@ -385,8 +405,21 @@
         return rtop[j, rows, :]
 
     flowing = early_down & (s == ns - 1)
-    middle = jnp.where(flowing, nz // 2, nz)
+    middle = jnp.where(flowing | ranked, nz // 2, nz)
     pl.loop(jnp.where(patient, nz, 0), middle)(one_layer)
+
+    @pl.when(ranked)
+    def _():
+        @pl.when(n_below < ns - 1)
+        def _():
+            pl.semaphore_wait(ok_slab, ns - 1 - n_below)
+
+        @pl.loop(s + 1, ns)
+        def _(peer):
+            top_copy(peer).start()
+
+        for copy, peer, exists in near:
+            pl.when(exists & is_above(peer))(copy.start)
 
     @pl.when(flowing)
     def _():
@@ -395,7 +428,7 @@
             cp_stage[j : j + 1, :] = cp_stage[j : j + 1, :] * top_rows(j, slice(R, R + 1))
 
     early_flow(flowing, 1)
-    pl.loop(middle, nz)(one_layer)
+    pl.loop(jnp.where(patient, nz, middle), nz)(one_layer)
 
     for c in range(H // 8):
         rows = slice(c * 8, c * 8 + 8)
@@ -417,14 +450,7 @@
 
     early_rows(early_down, 1)
     if half != 1:
-        early_rows(t == 1, 0)
-
-    pl.when(jnp.logical_not(flowing))(all_tops.wait_recv)
-
-    @pl.when(early_up & (s == 0))
-    def _():
-        for j in range(ns):
-            cm_stage[j : j + 1, :] = cm_stage[j : j + 1, :] * top_rows(j, slice(1, 2))
+        early_rows((t == 1) | (t == half - 1), 0)
 
     for copy in col_copies:
         copy.wait_recv()
@@ -442,6 +468,13 @@
             rows = slice(c * 8, c * 8 + 8)
             x = pltpu.roll(turned[rows], W - (2 * layer + 1), 1)
             out[layer, rows, :] = out[layer, rows, :] + jnp.where(rim_lane, x, 0.0)
+
+    pl.when(jnp.logical_not(flowing))(all_tops.wait_recv)
+
+    @pl.when(early_up & (s == 0))
+    def _():
+        for j in range(ns):
+            cm_stage[j : j + 1, :] = cm_stage[j : j + 1, :] * top_rows(j, slice(1, 2))
 
     @pl.when(s > 0)
     def _():
@@ -606,6 +639,7 @@
             dma((4,)),
             pltpu.SemaphoreType.REGULAR((2,)),
             pltpu.SemaphoreType.REGULAR((2,)),
+            pltpu.SemaphoreType.REGULAR,
         ],
         compiler_params=pltpu.CompilerParams(
             collective_id=0, has_side_effects=True, vmem_limit_bytes=56 * 1024 * 1024

time: 26.3 us -> 24.8 us (0.943)
  Pallas kernels: 24 us -> 22.6 us
    pallas_call x1, Pallas kernels: 24 us -> 22.6 us  [per_device(): pl.pallas_call(functools.partial(kernel, nt, ns, nz, H, R), out_shape=(vm...]
where the time goes in v4:
time: 24.8 us; the launch traced here: 24.7 us
  Pallas kernels  22.6 us (91%)
  local copies, waits for them, and re-layouts  1.47 us (6%)
  between operations  0.64 us (3%)
    pallas_call x1, Pallas kernels, per_device(): pl.pallas_call(functools.partial(kernel, nt, ns, nz, H, R), out_shape=(vm...  22.6 us
    unnamed x2, local copies, waits for them, and re-layouts  1.47 us

profile of v4, /device:TPU:2, one launch (start us, length us, event | category | flops | bytes accessed | tf_op | source)
XLA Modules:
  0.0 24.7 jit_solution(16543530372095821963)
XLA Ops:
  0.6 22.6 %shard_map.122 = (f32[10,128,128]{2,1,0:T(8,128)S(1)}, f32[4,4096]{1,0:T(4,128)S(1)}) custom-call(f32[10,128,128]{2,1,0:T(8,128)} %v_h.1, f32[10,128,128]{2,1,0:T(8,128)} %s_h.1, f32[10,128,128]{2,1,0:T(8,128)} %k_h.1, f32[10,128,128]{2,1,0:T(8,128)} %al_h.1, f32[10,128,128]{2,1,0:T(8,128)} %ph_h.1, f32[4,4096]{1,0:T(4,128)} %pond_h.1, f32[4,4096]{1,0:T(4,128)} %sx_h.1, ...), custom_call_target="tpu_custom_call" | custom-call | tf_op jit(solution)/shard_map/pallas_call | solution.py:586
  23.2 0.8 %copy.15 = f32[10,128,128]{2,1,0:T(8,128)} copy(f32[10,128,128]{2,1,0:T(8,128)S(1)} %get-tuple-element.2) | data formatting | bytes 1310720
  24.1 0.6 %copy.16 = f32[4,4096]{1,0:T(4,128)} copy(f32[4,4096]{1,0:T(4,128)S(1)} %get-tuple-element.3) | data formatting | bytes 131072

commit v5 on v4

--- a/solution.py
+++ b/solution.py
@@ -137,7 +137,6 @@
     def greet(tt, ss):
         pl.semaphore_signal(barrier, inc=1, device_id=(tt, ss), device_id_type=MESH)
 
-    n_y = ns // 4
     ranked = t == half - 1
     n_below = jnp.where(ranked, s, ns - 1)
 
@@ -275,10 +274,7 @@
             out[layer, rows, :] = total - flux
 
     patient = (t == 0) & (s > 0)
-    y = lax.rem(lax.div(s, 2), n_y)
-    last_started = (s >= ns // 2) & (y >= n_y // 2 - 1) & (y < n_y - 2)
-    prepared = patient | ((t == half - 1) & (s > 0) & jnp.logical_not(last_started))
-    prepared = prepared | (late_down & (s == ns - 1))
+    prepared = patient | (late_down & (s == ns - 1))
     pl.when(prepared)(local_rows)
     pl.when(prepared)(local_coefficients)
     pl.when(patient)(local_columns)

time: 24.8 us -> 24.8 us (level)
  no operation moved by 1% of the time
where the time goes in v5:
time: 24.8 us; the launch traced here: 24.7 us
  Pallas kernels  22.5 us (91%)
  local copies, waits for them, and re-layouts  1.47 us (6%)
  between operations  0.64 us (3%)
    pallas_call x1, Pallas kernels, per_device(): pl.pallas_call(functools.partial(kernel, nt, ns, nz, H, R), out_shape=(vm...  22.5 us
    unnamed x2, local copies, waits for them, and re-layouts  1.47 us

profile of v5, /device:TPU:2, one launch (start us, length us, event | category | flops | bytes accessed | tf_op | source)
XLA Modules:
  0.0 24.7 jit_solution(10271935806267313405)
XLA Ops:
  0.6 22.5 %shard_map.122 = (f32[10,128,128]{2,1,0:T(8,128)S(1)}, f32[4,4096]{1,0:T(4,128)S(1)}) custom-call(f32[10,128,128]{2,1,0:T(8,128)} %v_h.1, f32[10,128,128]{2,1,0:T(8,128)} %s_h.1, f32[10,128,128]{2,1,0:T(8,128)} %k_h.1, f32[10,128,128]{2,1,0:T(8,128)} %al_h.1, f32[10,128,128]{2,1,0:T(8,128)} %ph_h.1, f32[4,4096]{1,0:T(4,128)} %pond_h.1, f32[4,4096]{1,0:T(4,128)} %sx_h.1, ...), custom_call_target="tpu_custom_call" | custom-call | tf_op jit(solution)/shard_map/pallas_call | solution.py:582
  23.2 0.8 %copy.15 = f32[10,128,128]{2,1,0:T(8,128)} copy(f32[10,128,128]{2,1,0:T(8,128)S(1)} %get-tuple-element.2) | data formatting | bytes 1310720
  24.0 0.6 %copy.16 = f32[4,4096]{1,0:T(4,128)} copy(f32[4,4096]{1,0:T(4,128)S(1)} %get-tuple-element.3) | data formatting | bytes 131072
